TPU v7x, 512 devices: a whole 4x4x16 slice. The times are simulated.
512 devices in a mesh: tm: 32 (over z, core), ha: 4 (over y), wa: 4 (over x).
Axes of the slice: x: 4, y: 4, z: 16, core: 2. Of those that a mesh axis runs over, the one named last changes fastest.
Arguments:
- latents: bfloat16 [128, 48, 96, 16], P('tm', 'ha', 'wa'), may hold values from -6 to 6
- in_weight: bfloat16 [27, 16, 384], replicated, may hold values from -0.3125 to 0.3125
- in_bias: float32 [384], replicated, may hold values from -3 to 3
- norm_gain: float32 [384], replicated, may hold values from 0.1 to 1.9
- mid_weight: bfloat16 [27, 384, 256], replicated, may hold values from -0.0625 to 0.0625
- mid_bias: float32 [256], replicated, may hold values from -3 to 3
- row_heights: int32 [4], replicated, may hold values from 6 to 12, as said below
- col_widths: int32 [4], replicated, may hold values from 12 to 24, as said below
Outputs:
- features: bfloat16 [128, 48, 96, 256], P('tm', 'ha', 'wa')
Inputs may be any that keep to these rules, and one draw needn't show every extreme that they name: `row_heights`: the heights sum to 36; one tile row is exactly 12 rows high. `col_widths`: the widths sum to 72; one tile column is exactly 24 columns wide.
All inputs are finite; a program needn't handle non-finite values.
Results may differ from a plain program's by a relative error of at most 0.0051.
Values may be sent and summed in bfloat16 or wider, within the bound.
No kernel may reach another device: no remote copies, remote signals or barrier semaphores. Data moves between devices by JAX's collectives and lax.ppermute only.
A program may use at most 64 MiB of HBM per device.

v0:
```python
import jax
import jax.numpy as jnp
from jax import lax
from jax.sharding import PartitionSpec as P


def with_halo(cells, sides, width):
    for axis, dim in sides:
        count = lax.axis_size(axis)
        ends = count - 1
        head = lax.slice_in_dim(cells, 0, width, axis=dim)
        tail = lax.slice_in_dim(cells, cells.shape[dim] - width, cells.shape[dim], axis=dim)
        cells = jnp.concatenate(
            [
                lax.ppermute(tail, axis, [(i, (i + 1) % count) for i in range(ends)]),
                cells,
                lax.ppermute(head, axis, [((i + 1) % count, i) for i in range(ends)]),
            ],
            axis=dim,
        )
    return cells


def from_behind(shard, axis, by):
    devices = lax.axis_size(axis)
    pairs = [(i, i + by) for i in range(devices) if 0 <= i + by < devices]
    return lax.ppermute(shard, axis, pairs)


def conv_cells(field, kernel_taps):
    taps, inner, outer = kernel_taps.shape
    kernel = kernel_taps.reshape(3, 3, 3, inner, outer)
    return lax.conv_general_dilated(
        field[None],
        kernel,
        (1, 1, 1),
        "VALID",
        dimension_numbers=("NDHWC", "DHWIO", "NDHWC"),
        preferred_element_type=jnp.float32,
    )[0]


def activate(entry, norm_gain):
    values = entry.astype(jnp.float32)
    meansq = jnp.mean(values * values, axis=-1, keepdims=True)
    return jax.nn.silu(values * lax.rsqrt(meansq + 1e-06) * norm_gain).astype(jnp.bfloat16)


def with_rims(field, height, width):
    frames, rows, cols, chans = field.shape
    last_row = lax.dynamic_slice_in_dim(field, height - 1, 1, 1)
    edges = jnp.concatenate([field[:, :1], last_row], axis=1)
    got_rows = with_halo(edges, (("ha", 1),), 1)
    tall = jnp.concatenate(
        [got_rows[:, :1], field, jnp.zeros((frames, 1, cols, chans), field.dtype)], axis=1
    )
    tall = lax.dynamic_update_slice_in_dim(tall, got_rows[:, 3:4], height + 1, 1)
    last_col = lax.dynamic_slice_in_dim(tall, width - 1, 1, 2)
    sides = jnp.concatenate([tall[:, :, :1], last_col], axis=2)
    got_cols = with_halo(sides, (("wa", 2),), 1)
    wide = jnp.concatenate(
        [got_cols[:, :, :1], tall, jnp.zeros((frames, rows + 2, 1, chans), field.dtype)], axis=2
    )
    return lax.dynamic_update_slice_in_dim(wide, got_cols[:, :, 3:4], width + 1, 2)


def pick_entry(table, index):
    places = jnp.arange(table.shape[0], dtype=jnp.int32)
    return jnp.sum(jnp.where(places == index, table, 0))


def per_device(
    latents, in_weight, in_bias, norm_gain, mid_weight, mid_bias, row_heights, col_widths
):
    frames, rows, cols, zdim = latents.shape
    outer = mid_weight.shape[2]
    height = pick_entry(row_heights, lax.axis_index("ha"))
    width = pick_entry(col_widths, lax.axis_index("wa"))
    earlier = from_behind(latents[frames - 2 :], "tm", 1)
    latent_ext = jnp.concatenate([earlier, latents], axis=0)
    entry = (conv_cells(with_rims(latent_ext, height, width), in_weight) + in_bias).astype(
        jnp.bfloat16
    )
    active = activate(entry, norm_gain)
    carried = from_behind(active[frames - 2 :], "tm", 1)
    active_ext = jnp.concatenate([carried, active], axis=0)
    active_rim = with_rims(active_ext, height, width)
    mixed = conv_cells(active_rim, mid_weight)
    result = entry[..., :outer].astype(jnp.float32) + mixed + mid_bias
    row_ok = jnp.arange(rows, dtype=jnp.int32) < height
    col_ok = jnp.arange(cols, dtype=jnp.int32) < width
    keep = row_ok[:, None] & col_ok[None, :]
    return jnp.where(keep[None, :, :, None], result, 0.0).astype(jnp.bfloat16)


def solution(mesh):
    placed = (P("tm", "ha", "wa", None), P(), P(), P(), P(), P(), P(), P())
    return jax.shard_map(
        per_device, mesh=mesh, in_specs=placed, out_specs=P("tm", "ha", "wa", None), check_vma=False
    )
```

profile of v0, /device:TPU:128, one launch (start us, length us, event | category | flops | bytes accessed | tf_op | source)
XLA Modules:
  0.0 86.9 jit_solution(4689472227797842754)
XLA Ops:
  0.0 1.7 %copy.11 = bf16[4,12,24,16]{3,1,0,2:T(8,128)(2,1)S(1)} copy(bf16[4,12,24,16]{2,3,1,0:T(8,128)(2,1)} %param.8) | data formatting | bytes 73728 | tf_op args[0]
  1.7 1.9 %collective-permute-start = (bf16[2,12,24,16]{3,1,0,2:T(8,128)(2,1)S(1)}, bf16[2,12,24,16]{3,1,0,2:T(8,128)(2,1)S(1)}, u32[]{:S(2)}, u32[]{:S(2)}) collective-permute-start(bf16[2,12,24,16]{3,1,0,2:T(8,128)(2,1)S(1)} %slice.32), channel_id=1, source_target_pairs={{0,16},{16,32},{32,48},{48,64},{64,80},{80,96},{96,112},{112,128},... | collective-permute-start | bytes 55304 | tf_op jit(solution)/shard_map/ppermute | solution.py:27
  3.6 1.3 %fusion.34 = (s32[]{:T(128)}, s32[]{:T(128)}) fusion(s32[4]{0:T(128)} %param.14, s32[]{:T(128)S(6)} %axis_index.23, s32[4]{0:T(128)} %param.15, s32[]{:T(128)S(6)} %axis_index.25), kind=kLoop, calls=%fused_computation.57 | loop fusion | flops 22 | bytes 48 | tf_op jit(solution)/shard_map/reduce_sum | solution.py:69
  6.3 3.6 %collective-permute-done = bf16[2,12,24,16]{3,1,0,2:T(8,128)(2,1)S(1)} collective-permute-done((bf16[2,12,24,16]{3,1,0,2:T(8,128)(2,1)S(1)}, bf16[2,12,24,16]{3,1,0,2:T(8,128)(2,1)S(1)}, u32[]{:S(2)}, u32[]{:S(2)}) %collective-permute-start) | collective-permute-done | bytes 18464 | tf_op jit(solution)/shard_map/ppermute | solution.py:27
  10.1 3.5 %collective-permute-start.1 = (bf16[6,1,24,16]{3,1,0,2:T(2,128)(2,1)S(1)}, bf16[6,1,24,16]{3,1,0,2:T(2,128)(2,1)S(1)}, u32[]{:S(2)}, u32[]{:S(2)}) collective-permute-start(bf16[6,1,24,16]{3,1,0,2:T(2,128)(2,1)S(1)} %get-tuple-element.14), channel_id=1, source_target_pairs={{0,4},{4,8},{8,12},{1,5},{5,9},{9,13},{2,6},{6,10},{10,14},{3,7},{... | collective-permute-start | bytes 13832 | tf_op jit(solution)/shard_map/ppermute | solution.py:15
  16.2 1.3 %collective-permute-start.2 = (bf16[6,1,24,16]{3,1,0,2:T(2,128)(2,1)S(1)}, bf16[6,1,24,16]{3,1,0,2:T(2,128)(2,1)S(1)}, u32[]{:S(2)}, u32[]{:S(2)}) collective-permute-start(bf16[6,1,24,16]{3,1,0,2:T(2,128)(2,1)S(1)} %get-tuple-element.13), channel_id=1, source_target_pairs={{4,0},{8,4},{12,8},{5,1},{9,5},{13,9},{6,2},{10,6},{14,10},{7,3},{... | collective-permute-start | bytes 13832 | tf_op jit(solution)/shard_map/ppermute | solution.py:17
  17.9 4.6 %collective-permute-done.2 = bf16[6,1,24,16]{3,1,0,2:T(2,128)(2,1)S(1)} collective-permute-done((bf16[6,1,24,16]{3,1,0,2:T(2,128)(2,1)S(1)}, bf16[6,1,24,16]{3,1,0,2:T(2,128)(2,1)S(1)}, u32[]{:S(2)}, u32[]{:S(2)}) %collective-permute-start.2) | collective-permute-done | bytes 4640 | tf_op jit(solution)/shard_map/ppermute | solution.py:17
  22.5 2.3 %dynamic_update_slice.14 = bf16[6,14,24,16]{3,1,0,2:T(8,128)(2,1)S(1)} dynamic-update-slice(bf16[6,14,24,16]{3,1,0,2:T(8,128)(2,1)S(1)} %maximum_maximum_fusion.1, bf16[6,1,24,16]{3,1,0,2:T(2,128)(2,1)S(1)} %collective-permute-done.2, s32[]{:T(128)} %constant.13.clone.1, s32[]{:T(128)S(6)} %select_n.30, s32[]{:T(128)} %constant.13.clone.1, s32[]{:T(128)} %constant.13.clone.1) | dynamic-update-slice | bytes 9220 | tf_op jit(solution)/shard_map/dynamic_update_slice | solution.py:57
  24.8 3.4 %collective-permute-start.3 = (bf16[6,14,1,16]{3,1,0,2:T(8,128)(2,1)S(1)}, bf16[6,14,1,16]{3,1,0,2:T(8,128)(2,1)S(1)}, u32[]{:S(2)}, u32[]{:S(2)}) collective-permute-start(bf16[6,14,1,16]{3,1,0,2:T(8,128)(2,1)S(1)} %get-tuple-element.12), channel_id=1, source_target_pairs={{0,1},{1,2},{2,3},{4,5},{5,6},{6,7},{8,9},{9,10},{10,11},{12,13},{... | collective-permute-start | bytes 8072 | tf_op jit(solution)/shard_map/ppermute | solution.py:15
  29.5 1.3 %collective-permute-start.4 = (bf16[6,14,1,16]{3,1,0,2:T(8,128)(2,1)S(1)}, bf16[6,14,1,16]{3,1,0,2:T(8,128)(2,1)S(1)}, u32[]{:S(2)}, u32[]{:S(2)}) collective-permute-start(bf16[6,14,1,16]{3,1,0,2:T(8,128)(2,1)S(1)} %get-tuple-element.11), channel_id=1, source_target_pairs={{1,0},{2,1},{3,2},{5,4},{6,5},{7,6},{9,8},{10,9},{11,10},{13,12},{... | collective-permute-start | bytes 8072 | tf_op jit(solution)/shard_map/ppermute | solution.py:17
  31.0 4.2 %collective-permute-done.4 = bf16[6,14,1,16]{3,1,0,2:T(8,128)(2,1)S(1)} collective-permute-done((bf16[6,14,1,16]{3,1,0,2:T(8,128)(2,1)S(1)}, bf16[6,14,1,16]{3,1,0,2:T(8,128)(2,1)S(1)}, u32[]{:S(2)}, u32[]{:S(2)}) %collective-permute-start.4) | collective-permute-done | bytes 2720 | tf_op jit(solution)/shard_map/ppermute | solution.py:17
  36.0 1.7 %convolution_select_fusion = f32[4,12,8,4,384]{4,2,3,1,0:T(8,128)S(1)} fusion(bf16[3,3,3,16,384]{4,3,2,1,0:T(8,128)(2,1)S(1)} %bitcast.47, pred[8,4]{0,1:T(4,128)(4,1)S(1)} %copy-done.4, bf16[6,14,1,7,2,16]{5,3,4,1,0,2:T(8,128)(2,1)S(1)} %slice.34, bf16[6,14,1,8,4,16]{5,3,4,1,0,2:T(8,128)(2,1)S(1)} %copy.15), kind=kOutput, calls=%fused_computation.26 | convolution fusion | flops 510584832 | bytes 2814752 | tf_op jit(solution)/shard_map/conv_general_dilated | solution.py:33
  37.8 1.5 %copy.16 = f32[4,12,8,4,384]{4,0,3,2,1:T(4,128)S(1)} copy(f32[4,12,8,4,384]{4,2,3,1,0:T(8,128)S(1)} %convolution_select_fusion) | data formatting | bytes 4718592 | tf_op jit(solution)/shard_map/conv_general_dilated | solution.py:33
  40.0 1.2 %fusion.14 = bf16[4,12,24,384]{3,0,2,1:T(4,128)(2,1)S(1)} fusion(bf16[4,12,24,384]{3,0,2,1:T(4,128)(2,1)S(1)} %get-tuple-element.6, f32[384]{0:T(512)S(1)} %copy-done.2, f32[4,12,24]{0,2,1:T(8,128)S(1)} %add_rsqrt_fusion), kind=kLoop, calls=%fused_computation.20 | loop fusion | flops 3538944 | bytes 1775616 | tf_op jit(solution)/shard_map/convert_element_type | solution.py:46
  41.8 1.9 %collective-permute-start.5 = (bf16[2,12,24,384]{3,0,2,1:T(2,128)(2,1)S(1)}, bf16[2,12,24,384]{3,0,2,1:T(2,128)(2,1)S(1)}, u32[]{:S(2)}, u32[]{:S(2)}) collective-permute-start(bf16[2,12,24,384]{3,0,2,1:T(2,128)(2,1)S(1)} %slice.37), channel_id=1, source_target_pairs={{0,16},{16,32},{32,48},{48,64},{64,80},{80,96},{96,112},{112,128},... | collective-permute-start | bytes 1327112 | tf_op jit(solution)/shard_map/ppermute | solution.py:27
  44.3 8.3 %collective-permute-done.5 = bf16[2,12,24,384]{3,0,2,1:T(2,128)(2,1)S(1)} collective-permute-done((bf16[2,12,24,384]{3,0,2,1:T(2,128)(2,1)S(1)}, bf16[2,12,24,384]{3,0,2,1:T(2,128)(2,1)S(1)}, u32[]{:S(2)}, u32[]{:S(2)}) %collective-permute-start.5) | collective-permute-done | bytes 442400 | tf_op jit(solution)/shard_map/ppermute | solution.py:27
  52.7 3.5 %collective-permute-start.6 = (bf16[6,1,24,384]{3,0,2,1:T(8,128)(2,1)S(1)}, bf16[6,1,24,384]{3,0,2,1:T(8,128)(2,1)S(1)}, u32[]{:S(2)}, u32[]{:S(2)}) collective-permute-start(bf16[6,1,24,384]{3,0,2,1:T(8,128)(2,1)S(1)} %get-tuple-element.10), channel_id=1, source_target_pairs={{0,4},{4,8},{8,12},{1,5},{5,9},{9,13},{2,6},{6,10},{10,14},{3,7},{... | collective-permute-start | bytes 331784 | tf_op jit(solution)/shard_map/ppermute | solution.py:15
  56.9 1.3 %collective-permute-start.7 = (bf16[6,1,24,384]{3,0,2,1:T(8,128)(2,1)S(1)}, bf16[6,1,24,384]{3,0,2,1:T(8,128)(2,1)S(1)}, u32[]{:S(2)}, u32[]{:S(2)}) collective-permute-start(bf16[6,1,24,384]{3,0,2,1:T(8,128)(2,1)S(1)} %get-tuple-element.9), channel_id=1, source_target_pairs={{4,0},{8,4},{12,8},{5,1},{9,5},{13,9},{6,2},{10,6},{14,10},{7,3},{... | collective-permute-start | bytes 331784 | tf_op jit(solution)/shard_map/ppermute | solution.py:17
  58.9 1.1 %maximum_maximum_fusion = bf16[6,14,24,384]{3,0,2,1:T(8,128)(2,1)S(1)} fusion(bf16[4,12,24,384]{3,0,2,1:T(4,128)(2,1)S(1)} %fusion.14, bf16[2,12,24,384]{3,0,2,1:T(2,128)(2,1)S(1)} %collective-permute-done.5, bf16[6,1,24,384]{3,0,2,1:T(8,128)(2,1)S(1)} %collective-permute-done.6, bf16[14]{0:T(256)(128)(2,1)S(1)} %pad.23.clone), kind=kLoop, calls=%fused_computation.12 | loop fusion | flops 6193152 | bytes 2986012 | tf_op jit(solution)/shard_map/concatenate | solution.py:54
  60.0 4.0 %collective-permute-done.7 = bf16[6,1,24,384]{3,0,2,1:T(8,128)(2,1)S(1)} collective-permute-done((bf16[6,1,24,384]{3,0,2,1:T(8,128)(2,1)S(1)}, bf16[6,1,24,384]{3,0,2,1:T(8,128)(2,1)S(1)}, u32[]{:S(2)}, u32[]{:S(2)}) %collective-permute-start.7) | collective-permute-done | bytes 110624 | tf_op jit(solution)/shard_map/ppermute | solution.py:17
  64.0 3.4 %collective-permute-start.8 = (bf16[6,14,1,384]{3,0,2,1:T(8,128)(2,1)S(1)}, bf16[6,14,1,384]{3,0,2,1:T(8,128)(2,1)S(1)}, u32[]{:S(2)}, u32[]{:S(2)}) collective-permute-start(bf16[6,14,1,384]{3,0,2,1:T(8,128)(2,1)S(1)} %get-tuple-element.8), channel_id=1, source_target_pairs={{0,1},{1,2},{2,3},{4,5},{5,6},{6,7},{8,9},{9,10},{10,11},{12,13},{... | collective-permute-start | bytes 193544 | tf_op jit(solution)/shard_map/ppermute | solution.py:15
  67.5 1.5 %collective-permute-start.9 = (bf16[6,14,1,384]{3,0,2,1:T(8,128)(2,1)S(1)}, bf16[6,14,1,384]{3,0,2,1:T(8,128)(2,1)S(1)}, u32[]{:S(2)}, u32[]{:S(2)}) collective-permute-start(bf16[6,14,1,384]{3,0,2,1:T(8,128)(2,1)S(1)} %get-tuple-element.7), channel_id=1, source_target_pairs={{1,0},{2,1},{3,2},{5,4},{6,5},{7,6},{9,8},{10,9},{11,10},{13,12},{... | collective-permute-start | bytes 193544 | tf_op jit(solution)/shard_map/ppermute | solution.py:17
  70.1 3.7 %collective-permute-done.9 = bf16[6,14,1,384]{3,0,2,1:T(8,128)(2,1)S(1)} collective-permute-done((bf16[6,14,1,384]{3,0,2,1:T(8,128)(2,1)S(1)}, bf16[6,14,1,384]{3,0,2,1:T(8,128)(2,1)S(1)}, u32[]{:S(2)}, u32[]{:S(2)}) %collective-permute-start.9) | collective-permute-done | bytes 64544 | tf_op jit(solution)/shard_map/ppermute | solution.py:17
  75.5 8.9 %fusion.18 = f32[4,12,8,4,256]{4,2,3,1,0:T(8,128)S(1)} fusion(bf16[3,3,3,384,256]{4,3,2,1,0:T(8,128)(2,1)S(1)} %bitcast.54, bf16[6,14,1,7,2,384]{5,3,4,1,0,2:T(8,128)(2,1)S(1)} %slice.39, bf16[6,14,1,8,4,384]{5,3,4,1,0,2:T(8,128)(2,1)S(1)} %copy.21, pred[8,4]{0,1:T(4,128)(4,1)S(1)} %copy-done.4), kind=kOutput, calls=%fused_computation.28 | convolution fusion | flops 8163409920 | bytes 9848864 | tf_op jit(solution)/shard_map/conv_general_dilated | solution.py:33
  (47 shorter events, 10.3 us)
Async XLA Ops:
  0.0 36.0 %copy-start = (bf16[27,16,384]{2,1,0:T(8,128)(2,1)S(1)}, bf16[27,16,384]{2,1,0:T(8,128)(2,1)}, u32[]{:S(2)}) copy-start(bf16[27,16,384]{2,1,0:T(8,128)(2,1)} %param.9) | copy-start | bytes 995332
  1.7 8.2 %collective-permute-start = (bf16[2,12,24,16]{3,1,0,2:T(8,128)(2,1)S(1)}, bf16[2,12,24,16]{3,1,0,2:T(8,128)(2,1)S(1)}, u32[]{:S(2)}, u32[]{:S(2)}) collective-permute-start(bf16[2,12,24,16]{3,1,0,2:T(8,128)(2,1)S(1)} %slice.32), channel_id=1, source_target_pairs={{0,16},{16,32},{32,48},{48,64},{64,80},{80,96},{96,112},{112,128},... | collective-permute-start | bytes 55304 | tf_op jit(solution)/shard_map/ppermute | solution.py:27
  10.1 7.4 %collective-permute-start.1 = (bf16[6,1,24,16]{3,1,0,2:T(2,128)(2,1)S(1)}, bf16[6,1,24,16]{3,1,0,2:T(2,128)(2,1)S(1)}, u32[]{:S(2)}, u32[]{:S(2)}) collective-permute-start(bf16[6,1,24,16]{3,1,0,2:T(2,128)(2,1)S(1)} %get-tuple-element.14), channel_id=1, source_target_pairs={{0,4},{4,8},{8,12},{1,5},{5,9},{9,13},{2,6},{6,10},{10,14},{3,7},{... | collective-permute-start | bytes 13832 | tf_op jit(solution)/shard_map/ppermute | solution.py:15
  16.2 6.2 %collective-permute-start.2 = (bf16[6,1,24,16]{3,1,0,2:T(2,128)(2,1)S(1)}, bf16[6,1,24,16]{3,1,0,2:T(2,128)(2,1)S(1)}, u32[]{:S(2)}, u32[]{:S(2)}) collective-permute-start(bf16[6,1,24,16]{3,1,0,2:T(2,128)(2,1)S(1)} %get-tuple-element.13), channel_id=1, source_target_pairs={{4,0},{8,4},{12,8},{5,1},{9,5},{13,9},{6,2},{10,6},{14,10},{7,3},{... | collective-permute-start | bytes 13832 | tf_op jit(solution)/shard_map/ppermute | solution.py:17
  24.8 6.1 %collective-permute-start.3 = (bf16[6,14,1,16]{3,1,0,2:T(8,128)(2,1)S(1)}, bf16[6,14,1,16]{3,1,0,2:T(8,128)(2,1)S(1)}, u32[]{:S(2)}, u32[]{:S(2)}) collective-permute-start(bf16[6,14,1,16]{3,1,0,2:T(8,128)(2,1)S(1)} %get-tuple-element.12), channel_id=1, source_target_pairs={{0,1},{1,2},{2,3},{4,5},{5,6},{6,7},{8,9},{9,10},{10,11},{12,13},{... | collective-permute-start | bytes 8072 | tf_op jit(solution)/shard_map/ppermute | solution.py:15
  29.5 5.7 %collective-permute-start.4 = (bf16[6,14,1,16]{3,1,0,2:T(8,128)(2,1)S(1)}, bf16[6,14,1,16]{3,1,0,2:T(8,128)(2,1)S(1)}, u32[]{:S(2)}, u32[]{:S(2)}) collective-permute-start(bf16[6,14,1,16]{3,1,0,2:T(8,128)(2,1)S(1)} %get-tuple-element.11), channel_id=1, source_target_pairs={{1,0},{2,1},{3,2},{5,4},{6,5},{7,6},{9,8},{10,9},{11,10},{13,12},{... | collective-permute-start | bytes 8072 | tf_op jit(solution)/shard_map/ppermute | solution.py:17
  31.0 5.0 %copy-start.4 = (pred[8,4]{0,1:T(4,128)(4,1)S(1)}, pred[8,4]{0,1:T(4,128)(4,1)}, u32[]{:S(2)}) copy-start(pred[8,4]{0,1:T(4,128)(4,1)} %constant.52) | copy-start | bytes 100
  37.8 1.6 %copy-start.1 = (f32[384]{0:T(512)S(1)}, f32[384]{0:T(512)}, u32[]{:S(2)}) copy-start(f32[384]{0:T(512)} %param.10) | copy-start | bytes 4612
  39.3 0.7 copy-start.2
  41.8 10.8 %collective-permute-start.5 = (bf16[2,12,24,384]{3,0,2,1:T(2,128)(2,1)S(1)}, bf16[2,12,24,384]{3,0,2,1:T(2,128)(2,1)S(1)}, u32[]{:S(2)}, u32[]{:S(2)}) collective-permute-start(bf16[2,12,24,384]{3,0,2,1:T(2,128)(2,1)S(1)} %slice.37), channel_id=1, source_target_pairs={{0,16},{16,32},{32,48},{48,64},{64,80},{80,96},{96,112},{112,128},... | collective-permute-start | bytes 1327112 | tf_op jit(solution)/shard_map/ppermute | solution.py:27
  52.7 6.1 %collective-permute-start.6 = (bf16[6,1,24,384]{3,0,2,1:T(8,128)(2,1)S(1)}, bf16[6,1,24,384]{3,0,2,1:T(8,128)(2,1)S(1)}, u32[]{:S(2)}, u32[]{:S(2)}) collective-permute-start(bf16[6,1,24,384]{3,0,2,1:T(8,128)(2,1)S(1)} %get-tuple-element.10), channel_id=1, source_target_pairs={{0,4},{4,8},{8,12},{1,5},{5,9},{9,13},{2,6},{6,10},{10,14},{3,7},{... | collective-permute-start | bytes 331784 | tf_op jit(solution)/shard_map/ppermute | solution.py:15
  56.9 7.0 %collective-permute-start.7 = (bf16[6,1,24,384]{3,0,2,1:T(8,128)(2,1)S(1)}, bf16[6,1,24,384]{3,0,2,1:T(8,128)(2,1)S(1)}, u32[]{:S(2)}, u32[]{:S(2)}) collective-permute-start(bf16[6,1,24,384]{3,0,2,1:T(8,128)(2,1)S(1)} %get-tuple-element.9), channel_id=1, source_target_pairs={{4,0},{8,4},{12,8},{5,1},{9,5},{13,9},{6,2},{10,6},{14,10},{7,3},{... | collective-permute-start | bytes 331784 | tf_op jit(solution)/shard_map/ppermute | solution.py:17
  64.0 5.5 %collective-permute-start.8 = (bf16[6,14,1,384]{3,0,2,1:T(8,128)(2,1)S(1)}, bf16[6,14,1,384]{3,0,2,1:T(8,128)(2,1)S(1)}, u32[]{:S(2)}, u32[]{:S(2)}) collective-permute-start(bf16[6,14,1,384]{3,0,2,1:T(8,128)(2,1)S(1)} %get-tuple-element.8), channel_id=1, source_target_pairs={{0,1},{1,2},{2,3},{4,5},{5,6},{6,7},{8,9},{9,10},{10,11},{12,13},{... | collective-permute-start | bytes 193544 | tf_op jit(solution)/shard_map/ppermute | solution.py:15
  67.5 6.4 %collective-permute-start.9 = (bf16[6,14,1,384]{3,0,2,1:T(8,128)(2,1)S(1)}, bf16[6,14,1,384]{3,0,2,1:T(8,128)(2,1)S(1)}, u32[]{:S(2)}, u32[]{:S(2)}) collective-permute-start(bf16[6,14,1,384]{3,0,2,1:T(8,128)(2,1)S(1)} %get-tuple-element.7), channel_id=1, source_target_pairs={{1,0},{2,1},{3,2},{5,4},{6,5},{7,6},{9,8},{10,9},{11,10},{13,12},{... | collective-permute-start | bytes 193544 | tf_op jit(solution)/shard_map/ppermute | solution.py:17
  69.5 6.0 %slice-start = ((s8[5308416]{0:T(1024)(128)(4,1)}), s8[4194304]{0:T(1024)(128)(4,1)S(1)}, s32[]{:S(2)}) async-start(s8[5308416]{0:T(1024)(128)(4,1)} %bitcast.52), calls=%async_computation | async-start | bytes 8388608
  73.9 1.6 %slice-start.1 = ((s8[5308416]{0:T(1024)(128)(4,1)}), s8[1114112]{0:T(1024)(128)(4,1)S(1)}, s32[]{:S(2)}) async-start(s8[5308416]{0:T(1024)(128)(4,1)} %bitcast.52), calls=%async_computation.1 | async-start | bytes 2228224
  84.4 1.1 %copy-start.3 = (f32[256]{0:T(256)S(1)}, f32[256]{0:T(256)}, u32[]{:S(2)}) copy-start(f32[256]{0:T(256)} %param.13) | copy-start | bytes 3076
where the time goes:
time: 87.4 us; the launch traced here: 86.9 us
  waiting for transfers between devices  29.6 us (34%)
  starting transfers between devices  22.9 us (26%)
  matrix products  10.7 us (12%)
  local copies, waits for them, and re-layouts  10.4 us (12%)
  other arithmetic  7.76 us (9%)
  between operations  5.53 us (6%)
    ppermute x4, waiting for transfers between devices, with_halo(): lax.ppermute(head, axis, [((i + 1) % count, i) for i in range(ends)])  16.5 us
    ppermute x4, starting transfers between devices, with_halo(): lax.ppermute(tail, axis, [(i, (i + 1) % count) for i in range(ends)])  13.8 us
    ppermute x2, waiting for transfers between devices, from_behind(): return lax.ppermute(shard, axis, pairs)  11.9 us
    conv_general_dilated x2, matrix products, conv_cells(): lax.conv_general_dilated(field[None], kernel, (1, 1, 1), 'VALID', dimensi...  10.7 us
    ppermute x4, starting transfers between devices, with_halo(): lax.ppermute(head, axis, [((i + 1) % count, i) for i in range(ends)])  5.33 us
    conv_general_dilated x6, local copies, waits for them, and re-layouts, conv_cells(): lax.conv_general_dilated(field[None], kernel, (1, 1, 1), 'VALID', dimensi...  4.11 us
    ppermute x2, starting transfers between devices, from_behind(): return lax.ppermute(shard, axis, pairs)  3.84 us
    dynamic_update_slice x2, local copies, waits for them, and re-layouts, with_rims(): lax.dynamic_update_slice_in_dim(tall, got_rows[:, 3:4], height + 1, 1)  2.32 us
  transfers between devices with their start and end apart: 10, of which 8 were waited for; matrix products, arithmetic and copies ran while one was open for 6% of the time, Pallas kernels for 0%

commit v1 on v0

v1 whole, which is shorter than its diff:
```python
import jax
import jax.numpy as jnp
from jax import lax
from jax.experimental import pallas as pl
from jax.experimental.pallas import tpu as pltpu
from jax.sharding import PartitionSpec as P

F = 4
TH, TW = 12, 24
Z, C, CO = 16, 384, 256
NH, NW = 4, 4
LANES = 128
SPAN = 32
RE = TH + 4
RA = TH + 2
MR = F * TW

VM = pltpu.MemorySpace.VMEM
SM = pltpu.MemorySpace.SMEM


def lanes_of():
    return lax.broadcasted_iota(jnp.int32, (Z, LANES), 1) % SPAN


def pack_kernel(rh_ref, cw_ref, lat_ref, blocks_ref, own_ref, f32_ref):
    i, j = lax.axis_index("ha"), lax.axis_index("wa")
    h, w = rh_ref[i], cw_ref[j]
    lane = lanes_of()
    blocks_ref[...] = jnp.zeros_like(blocks_ref)
    f32_ref[...] = jnp.zeros_like(f32_ref)
    for r in range(TH):
        for f in range(F):
            f32_ref[2 + r, :, f * SPAN + 2 : f * SPAN + 2 + TW] = lat_ref[f, r].astype(jnp.float32)
    right = jnp.zeros((Z, LANES), jnp.float32)
    left = jnp.zeros((Z, LANES), jnp.float32)
    for r in range(TH):
        row = f32_ref[2 + r]
        here = (lane // 2) == r
        right = jnp.where(here, pltpu.roll(row, 2 * r - w + LANES, 1), right)
        left = jnp.where(here, pltpu.roll(row, (2 * r - 2) % LANES, 1), left)
    right = right.astype(jnp.bfloat16)
    left = left.astype(jnp.bfloat16)
    own_ref[...] = f32_ref[...].astype(jnp.bfloat16)
    for di in (-1, 0, 1):
        row_in = (i + di >= 0) & (i + di < NH)
        for dj, tile in ((-1, left), (1, right)):
            @pl.when(row_in & (j + dj >= 0) & (j + dj < NW))
            def _(di=di, dj=dj, tile=tile):
                blocks_ref[(i + di) * NW + j + dj, 0:Z] = tile

    @pl.when(i > 0)
    def _():
        for k in range(2):
            blocks_ref[(i - 1) * NW + j, k * Z : (k + 1) * Z] = f32_ref[2 + k].astype(jnp.bfloat16)

    @pl.when(i < NH - 1)
    def _():
        for k in range(2):
            blocks_ref[(i + 1) * NW + j, k * Z : (k + 1) * Z] = f32_ref[h + k].astype(jnp.bfloat16)


def join_kernel(rh_ref, cw_ref, got_ref, own_ref, ext_ref, f32_ref):
    i, j = lax.axis_index("ha"), lax.axis_index("wa")
    h, w = rh_ref[i], cw_ref[j]
    up, down = jnp.maximum(i - 1, 0), jnp.minimum(i + 1, NH - 1)
    hu = rh_ref[up]
    lane = lanes_of()
    to_left, to_right = lane < 2, (lane >= w + 2) & (lane < w + 4)

    def strip(at, k, ok):
        return jnp.where(ok, got_ref[at, k * Z : (k + 1) * Z].astype(jnp.float32), 0.0)

    def sides(row):
        out = []
        for col, ok in ((jnp.maximum(j - 1, 0), j > 0), (jnp.minimum(j + 1, NW - 1), j < NW - 1)):
            row_ok = ok & (row >= 0) & (row < NH)
            out.append(strip(jnp.clip(row, 0, NH - 1) * NW + col, 0, row_ok))
        return out

    def put(at, base, pair, r):
        row = jnp.where(to_left, pltpu.roll(pair[0], LANES - 2 * r, 1), base)
        row = jnp.where(to_right, pltpu.roll(pair[1], LANES + w + 2 - 2 * r, 1), row)
        f32_ref[at] = row

    mid = sides(i)
    for r in range(TH):
        put(2 + r, own_ref[2 + r].astype(jnp.float32), mid, r)
    above, below = sides(i - 1), sides(i + 1)
    for k in range(2):
        put(k, strip(up * NW + j, k, i > 0), above, hu - 2 + k)
    for k in range(2):
        put(h + 2 + k, strip(down * NW + j, k, i < NH - 1), below, k)
    ext_ref[...] = f32_ref[...].astype(jnp.bfloat16)


def main_kernel(
    rh_ref, cw_ref, prev_ref, own_ref, wi_ref, bi_ref, gain_ref, wm_ref, bm_ref,
    out_ref, sa_ref, sb_ref, lhs_ref, short_ref, acc_ref,
):
    t, i, j = lax.axis_index("tm"), lax.axis_index("ha"), lax.axis_index("wa")
    h, w = rh_ref[i], cw_ref[j]
    lane = lax.broadcasted_iota(jnp.int32, (Z, LANES), 1)

    def taps(field, ref, at):
        for dc in range(3):
            piece = field if dc == 0 else pltpu.roll(field, LANES - dc, 1)
            ref[at + dc * Z : at + (dc + 1) * Z] = piece.astype(jnp.bfloat16)

    for r in range(RE):
        prev, own = prev_ref[r].astype(jnp.float32), own_ref[r].astype(jnp.float32)
        one = jnp.where(lane < 3 * SPAN, pltpu.roll(prev, 3 * SPAN, 1), pltpu.roll(own, 3 * SPAN, 1))
        two = jnp.where(lane < 2 * SPAN, pltpu.roll(prev, 2 * SPAN, 1), pltpu.roll(own, 2 * SPAN, 1))
        for dt, field in enumerate((prev, one, two)):
            taps(field, sa_ref, (r * 9 + dt * 3) * Z)
    for r in range(RE - 1):
        own = own_ref[r].astype(jnp.float32)
        nxt = own_ref[r + 1].astype(jnp.float32)
        for dt in range(3):
            a = own if dt == 0 else pltpu.roll(own, LANES - dt * SPAN, 1)
            b = nxt if dt == 2 else pltpu.roll(nxt, (2 - dt) * SPAN, 1)
            taps(jnp.where(lane < 2 * SPAN, a, b), sb_ref, (r * 9 + dt * 3) * Z)

    bias, gain = bi_ref[...], gain_ref[...]
    pos = lax.broadcasted_iota(jnp.int32, (LANES, 1), 0)
    col = pos % SPAN
    col_ok = ((j > 0) | (col > 0)) & ((j < NW - 1) | (col <= w))
    early = (t > 0) | (pos >= 2 * SPAN)

    def row_ok(r):
        return ((i > 0) | (r > 0)) & ((i < NH - 1) | (r <= h))

    def entry_of(s):
        got = lax.dot_general(
            s, wi_ref[...], (((0,), (0,)), ((), ())), preferred_element_type=jnp.float32
        )
        return (got + bias).astype(jnp.bfloat16).astype(jnp.float32)

    def active_of(entry, ok):
        meansq = jnp.mean(entry * entry, axis=-1, keepdims=True)
        v = entry * jnp.where(ok, lax.rsqrt(meansq + 1e-06), 0.0) * gain
        half = 0.5 * v
        return half + half * jnp.tanh(half)

    def step(q, _):
        r = 2 * q
        ents, acts = [], []
        for k in range(2):
            at = pl.multiple_of((r + k) * 9 * Z, Z)
            e = entry_of(sa_ref[pl.ds(at, 27 * Z), :])
            ents.append(e)
            acts.append(active_of(e, col_ok & early & row_ok(r + k)))
        at = pl.multiple_of(r * 9 * Z, Z)
        e = entry_of(sb_ref[pl.ds(at, 27 * Z), :])
        b = active_of(e, col_ok & ((row_ok(r) & (pos < 2 * SPAN)) | (row_ok(r + 1) & (pos >= 2 * SPAN))))
        for k in range(2):
            frames = [acts[k][f * SPAN : (f + 1) * SPAN] for f in range(4)]
            frames += [b[(2 * k + f) * SPAN : (2 * k + f + 1) * SPAN] for f in range(2)]
            m = pl.multiple_of((r + k) * MR, 16)
            for dc in range(3):
                cut = [a[dc : dc + TW] for a in frames]
                for dt in range(3):
                    lhs_ref[pl.ds(m, MR), (dt * 3 + dc) * C : (dt * 3 + dc + 1) * C] = (
                        jnp.concatenate(cut[dt : dt + 4], axis=0).astype(jnp.bfloat16)
                    )
            ef = [ents[k][(2 + f) * SPAN : (3 + f) * SPAN, :CO] for f in range(2)]
            ef += [e[(2 * k + f) * SPAN : (2 * k + f + 1) * SPAN, :CO] for f in range(2)]
            short_ref[pl.ds(m, MR), :] = jnp.concatenate([a[1 : 1 + TW] for a in ef], axis=0)
        return 0

    lax.fori_loop(0, RA // 2, step, 0)

    for dt in range(3):
        for dr in range(3):
            tap = 9 * dt + 3 * dr
            got = jnp.dot(
                lhs_ref[dr * MR : dr * MR + TH * MR, dt * 3 * C : (dt + 1) * 3 * C],
                wm_ref[tap : tap + 3].reshape(3 * C, CO),
                preferred_element_type=jnp.float32,
            )
            if dt == dr == 0:
                acc_ref[...] = got
            else:
                acc_ref[...] += got

    bias_m = bm_ref[...]
    keep_col = lax.broadcasted_iota(jnp.int32, (TW, 1), 0) < w
    for r in range(TH):
        ok = keep_col & (r < h)
        for f in range(F):
            m = r * MR + f * TW
            val = short_ref[m + MR : m + MR + TW] + acc_ref[m : m + TW] + bias_m
            out_ref[f, r] = jnp.where(ok, val, 0.0).astype(jnp.bfloat16)


def per_device(
    latents, in_weight, in_bias, norm_gain, mid_weight, mid_bias, row_heights, col_widths
):
    flipped = jnp.transpose(latents, (0, 1, 3, 2))
    smem, vmem = pl.BlockSpec(memory_space=SM), pl.BlockSpec(memory_space=VM)
    bf16, f32 = jnp.bfloat16, jnp.float32
    blocks, own = pl.pallas_call(
        pack_kernel,
        out_shape=(
            jax.ShapeDtypeStruct((NH * NW, 2 * Z, LANES), bf16),
            jax.ShapeDtypeStruct((RE, Z, LANES), bf16),
        ),
        in_specs=[smem, smem, vmem],
        out_specs=(vmem, vmem),
        scratch_shapes=[pltpu.VMEM((RE, Z, LANES), f32)],
    )(row_heights, col_widths, flipped)
    got = lax.all_to_all(blocks, ("ha", "wa"), 0, 0, tiled=True)
    ext = pl.pallas_call(
        join_kernel,
        out_shape=jax.ShapeDtypeStruct((RE, Z, LANES), bf16),
        in_specs=[smem, smem, vmem, vmem],
        out_specs=vmem,
        scratch_shapes=[pltpu.VMEM((RE, Z, LANES), f32)],
    )(row_heights, col_widths, got, own)
    groups = lax.axis_size("tm")
    prev = lax.ppermute(ext, "tm", [(g, g + 1) for g in range(groups - 1)])
    wi = in_weight.reshape(3, 3, 3, Z, C).transpose(1, 0, 2, 3, 4).reshape(27 * Z, C)
    return pl.pallas_call(
        main_kernel,
        out_shape=jax.ShapeDtypeStruct((F, TH, TW, CO), bf16),
        in_specs=[smem, smem] + [vmem] * 7,
        out_specs=vmem,
        scratch_shapes=[
            pltpu.VMEM((RE * 9 * Z, LANES), bf16),
            pltpu.VMEM((RE * 9 * Z, LANES), bf16),
            pltpu.VMEM((RA * MR, 9 * C), bf16),
            pltpu.VMEM((RA * MR, CO), f32),
            pltpu.VMEM((TH * MR, CO), f32),
        ],
        compiler_params=pltpu.CompilerParams(vmem_limit_bytes=48 * 1024 * 1024),
    )(
        row_heights, col_widths, prev, ext, wi, in_bias.reshape(1, C), norm_gain.reshape(1, C),
        mid_weight, mid_bias.reshape(1, CO),
    )


def solution(mesh):
    placed = (P("tm", "ha", "wa", None), P(), P(), P(), P(), P(), P(), P())
    return jax.shard_map(
        per_device, mesh=mesh, in_specs=placed, out_specs=P("tm", "ha", "wa", None), check_vma=False
    )
```

time: 87.4 us -> 49.1 us (0.56)
  the two profiles are of different devices: /device:TPU:128 before, /device:TPU:225 now
where the time goes in v1:
time: 49.1 us; the launch traced here: 48.7 us
  Pallas kernels  20.5 us (42%)
  blocking collectives  13.7 us (28%)
  local copies, waits for them, and re-layouts  7.7 us (16%)
  starting transfers between devices  6.71 us (14%)
    pallas_call x1, Pallas kernels, per_device(): pl.pallas_call(main_kernel, out_shape=jax.ShapeDtypeStruct((F, TH, TW, CO...  17 us
    all_to_all x1, blocking collectives, per_device(): got = lax.all_to_all(blocks, ('ha', 'wa'), 0, 0, tiled=True)  13.7 us
    ppermute x1, starting transfers between devices, per_device(): prev = lax.ppermute(ext, 'tm', [(g, g + 1) for g in range(groups - 1)])  6.71 us
    unnamed x10, local copies, waits for them, and re-layouts  5.33 us
    pallas_call x1, Pallas kernels, per_device(): pl.pallas_call(pack_kernel, out_shape=(jax.ShapeDtypeStruct((NH * NW, 2 *...  1.83 us
    pallas_call x1, Pallas kernels, per_device(): pl.pallas_call(join_kernel, out_shape=jax.ShapeDtypeStruct((RE, Z, LANES)...  1.67 us
    reshape x1, local copies, waits for them, and re-layouts, per_device(): in_weight.reshape(3, 3, 3, Z, C).transpose(1, 0, 2, 3, 4).reshape(27 * Z, C)  1.01 us
  transfers between devices with their start and end apart: 1, of which 0 were waited for; matrix products, arithmetic and copies ran while one was open for 5% of the time, Pallas kernels for 0%

profile of v1, /device:TPU:225, one launch (start us, length us, event | category | flops | bytes accessed | tf_op | source)
XLA Modules:
  0.0 48.7 jit_solution(16279695150749436656)
XLA Ops:
  0.0 1.8 %shard_map.82 = (bf16[16,32,128]{2,1,0:T(8,128)(2,1)}, bf16[16,16,128]{2,1,0:T(8,128)(2,1)}) custom-call(s32[4]{0:T(128)} %rh_ref.5, s32[4]{0:T(128)} %cw_ref.5, bf16[4,12,16,24]{3,2,1,0:T(8,128)(2,1)} %bitcast.9), custom_call_target="tpu_custom_call" | custom-call | tf_op jit(solution)/shard_map/pallas_call | solution.py:202
  1.8 13.7 %all_to_all.5.got_ref = bf16[16,32,128]{2,1,0:T(8,128)(2,1)} all-to-all(bf16[16,32,128]{2,1,0:T(8,128)(2,1)} %get-tuple-element.7), channel_id=1, replica_groups=mesh['tm'=32,'ha'=4,'wa'=4] {'ha','wa'}, dimensions={0} | all-to-all | bytes 262144 | tf_op jit(solution)/shard_map/all_to_all | solution.py:212
  15.6 1.7 %shard_map.83.own_ref = bf16[16,16,128]{2,1,0:T(8,128)(2,1)} custom-call(s32[4]{0:T(128)} %rh_ref.5, s32[4]{0:T(128)} %cw_ref.5, bf16[16,32,128]{2,1,0:T(8,128)(2,1)} %all_to_all.5.got_ref, bf16[16,16,128]{2,1,0:T(8,128)(2,1)} %get-tuple-element.8.own_ref), custom_call_target="tpu_custom_call" | custom-call | tf_op jit(solution)/shard_map/pallas_call | solution.py:213
  17.2 6.7 %collective-permute-start = (bf16[16,16,128]{2,1,0:T(8,128)(2,1)}, bf16[16,16,128]{2,1,0:T(8,128)(2,1)S(1)}, u32[]{:S(2)}, u32[]{:S(2)}) collective-permute-start(bf16[16,16,128]{2,1,0:T(8,128)(2,1)} %shard_map.83.own_ref), channel_id=1, source_target_pairs={{0,16},{16,32},{32,48},{48,64},{64,80},{80,96},{96,112},{112,128},... | collective-permute-start | bytes 196616 | tf_op jit(solution)/shard_map/ppermute | solution.py:221
  23.9 0.7 %reshape.17.bi_ref = f32[1,384]{1,0:T(1,128)S(1)} reshape(f32[384]{0:T(512)} %param.10) | data formatting | bytes 3072 | tf_op jit(solution)/shard_map/reshape | solution.py:237
  24.6 0.7 %reshape.18.gain_ref = f32[1,384]{1,0:T(1,128)S(1)} reshape(f32[384]{0:T(512)} %param.11) | data formatting | bytes 3072 | tf_op jit(solution)/shard_map/reshape | solution.py:237
  25.3 1.0 %copy.9 = bf16[3,3,3,16,384]{4,3,2,0,1:T(8,128)(2,1)S(1)} copy(bf16[3,3,3,16,384]{4,3,2,1,0:T(8,128)(2,1)} %bitcast.8) | data formatting | bytes 663552 | tf_op jit(solution)/shard_map/reshape | solution.py:222
  26.3 0.0 collective-permute-done.prev_ref
  26.3 0.0 copy-start
  26.3 2.5 %copy-done = bf16[27,384,256]{2,1,0:T(8,128)(2,1)S(1)} copy-done((bf16[27,384,256]{2,1,0:T(8,128)(2,1)S(1)}, bf16[27,384,256]{2,1,0:T(8,128)(2,1)}, u32[]{:S(2)}) %copy-start) | copy-done | bytes 5308440
  28.8 0.0 copy-start.1
  28.8 0.8 %copy-done.1 = bf16[16,16,128]{2,1,0:T(8,128)(2,1)S(1)} copy-done((bf16[16,16,128]{2,1,0:T(8,128)(2,1)S(1)}, bf16[16,16,128]{2,1,0:T(8,128)(2,1)}, u32[]{:S(2)}) %copy-start.1) | copy-done | bytes 65560
  29.7 0.0 copy-start.2
  29.7 0.7 %copy-done.2 = s32[4]{0:T(128)S(1)} copy-done((s32[4]{0:T(128)S(1)}, s32[4]{0:T(128)}, u32[]{:S(2)}) %copy-start.2) | copy-done | bytes 40
  30.3 0.0 copy-start.3
  30.3 0.7 %copy-done.3 = s32[4]{0:T(128)S(1)} copy-done((s32[4]{0:T(128)S(1)}, s32[4]{0:T(128)}, u32[]{:S(2)}) %copy-start.3) | copy-done | bytes 40
  31.0 0.0 copy-start.4
  31.0 0.7 %copy-done.4 = f32[256]{0:T(256)S(1)} copy-done((f32[256]{0:T(256)S(1)}, f32[256]{0:T(256)}, u32[]{:S(2)}) %copy-start.4) | copy-done | bytes 1048
  31.7 17.0 %shard_map.84 = bf16[4,12,24,256]{3,2,1,0:T(8,128)(2,1)} custom-call(s32[4]{0:T(128)S(1)} %copy-done.2, s32[4]{0:T(128)S(1)} %copy-done.3, bf16[16,16,128]{2,1,0:T(8,128)(2,1)S(1)} %collective-permute-done.prev_ref, bf16[16,16,128]{2,1,0:T(8,128)(2,1)S(1)} %copy-done.1, bf16[432,384]{1,0:T(8,128)(2,1)S(1)} %bitcast.6, f32[1,384]{1,0:T(1,128)S(1)} %reshape.17.bi_ref, ...), custom_call_target="tpu_custom_call" | custom-call | tf_op jit(solution)/shard_map/pallas_call | solution.py:223
Async XLA Ops:
  17.2 9.1 %collective-permute-start = (bf16[16,16,128]{2,1,0:T(8,128)(2,1)}, bf16[16,16,128]{2,1,0:T(8,128)(2,1)S(1)}, u32[]{:S(2)}, u32[]{:S(2)}) collective-permute-start(bf16[16,16,128]{2,1,0:T(8,128)(2,1)} %shard_map.83.own_ref), channel_id=1, source_target_pairs={{0,16},{16,32},{32,48},{48,64},{64,80},{80,96},{96,112},{112,128},... | collective-permute-start | bytes 196616 | tf_op jit(solution)/shard_map/ppermute | solution.py:221
  26.3 2.5 %copy-start = (bf16[27,384,256]{2,1,0:T(8,128)(2,1)S(1)}, bf16[27,384,256]{2,1,0:T(8,128)(2,1)}, u32[]{:S(2)}) copy-start(bf16[27,384,256]{2,1,0:T(8,128)(2,1)} %wm_ref.1) | copy-start | bytes 15925252
  28.8 0.8 %copy-start.1 = (bf16[16,16,128]{2,1,0:T(8,128)(2,1)S(1)}, bf16[16,16,128]{2,1,0:T(8,128)(2,1)}, u32[]{:S(2)}) copy-start(bf16[16,16,128]{2,1,0:T(8,128)(2,1)} %shard_map.83.own_ref) | copy-start | bytes 196612
  29.7 0.7 %copy-start.2 = (s32[4]{0:T(128)S(1)}, s32[4]{0:T(128)}, u32[]{:S(2)}) copy-start(s32[4]{0:T(128)} %rh_ref.5) | copy-start | bytes 52
  30.3 0.7 %copy-start.3 = (s32[4]{0:T(128)S(1)}, s32[4]{0:T(128)}, u32[]{:S(2)}) copy-start(s32[4]{0:T(128)} %cw_ref.5) | copy-start | bytes 52
  31.0 0.7 %copy-start.4 = (f32[256]{0:T(256)S(1)}, f32[256]{0:T(256)}, u32[]{:S(2)}) copy-start(f32[256]{0:T(256)} %param.13) | copy-start | bytes 3076

commit v2 on v1

v2 whole, which is shorter than its diff:
```python
import jax
import jax.numpy as jnp
from jax import lax
from jax.experimental import pallas as pl
from jax.experimental.pallas import tpu as pltpu
from jax.sharding import PartitionSpec as P

F = 4
TH, TW = 12, 24
Z, C, CO = 16, 384, 256
NH, NW = 4, 4
LANES = 128
SPAN = 32
RE = TH + 4
RA = TH + 2
MR = F * TW
HALF = TH // 2
PR = 2 * TW

VM = pltpu.MemorySpace.VMEM
HBM = pltpu.MemorySpace.HBM


def lanes_of():
    return lax.broadcasted_iota(jnp.int32, (Z, LANES), 1) % SPAN


def name(pairs, sems):
    return [pltpu.make_async_copy(src, dst, sems.at[k]) for k, (src, dst) in enumerate(pairs)]


def fetch(pairs, sems):
    copies = name(pairs, sems)
    for copy in copies:
        copy.start()
    return copies


def pack_kernel(
    rh_hbm, cw_hbm, lat_hbm, blocks_ref, own_ref, f32_ref, lat_ref, rh_ref, cw_ref, sems
):
    copies = fetch(((rh_hbm, rh_ref), (cw_hbm, cw_ref), (lat_hbm, lat_ref)), sems)
    i, j = lax.axis_index("ha"), lax.axis_index("wa")
    lane = lanes_of()
    blocks_ref[...] = jnp.zeros_like(blocks_ref)
    f32_ref[...] = jnp.zeros_like(f32_ref)
    for copy in copies:
        copy.wait()
    h, w = rh_ref[i], cw_ref[j]
    for r in range(TH):
        for f in range(F):
            f32_ref[2 + r, :, f * SPAN + 2 : f * SPAN + 2 + TW] = lat_ref[f, r].astype(jnp.float32)
    right = jnp.zeros((Z, LANES), jnp.float32)
    left = jnp.zeros((Z, LANES), jnp.float32)
    for r in range(TH):
        row = f32_ref[2 + r]
        here = (lane // 2) == r
        right = jnp.where(here, pltpu.roll(row, (2 * r - w + LANES) % LANES, 1), right)
        left = jnp.where(here, pltpu.roll(row, (2 * r - 2) % LANES, 1), left)
    right = right.astype(jnp.bfloat16)
    left = left.astype(jnp.bfloat16)
    own_ref[...] = f32_ref[...].astype(jnp.bfloat16)
    for di in (-1, 0, 1):
        row_in = (i + di >= 0) & (i + di < NH)
        for dj, tile in ((-1, left), (1, right)):
            @pl.when(row_in & (j + dj >= 0) & (j + dj < NW))
            def _(di=di, dj=dj, tile=tile):
                blocks_ref[(i + di) * NW + j + dj, 0:Z] = tile

    @pl.when(i > 0)
    def _():
        for k in range(2):
            blocks_ref[(i - 1) * NW + j, k * Z : (k + 1) * Z] = f32_ref[2 + k].astype(jnp.bfloat16)

    @pl.when(i < NH - 1)
    def _():
        for k in range(2):
            blocks_ref[(i + 1) * NW + j, k * Z : (k + 1) * Z] = f32_ref[h + k].astype(jnp.bfloat16)


def name_weights(sources, outs, scratch):
    wm_hbm, wi_hbm, bi_hbm, gain_hbm, bm_hbm = sources
    u_ref, wi_ref, bi_ref, gain_ref, bm_ref = outs
    mid_ref, wi_raw, sems = scratch
    small = name(
        ((wi_hbm, wi_raw), (bi_hbm, bi_ref), (gain_hbm, gain_ref), (bm_hbm, bm_ref)), sems
    )
    copies = []
    for g in range(3):
        part = pl.ds(g * 3, 3)
        homes = (u_ref.at[0, part], mid_ref.at[part], u_ref.at[3, part])
        copies += name(
            [(wm_hbm.at[pl.ds(9 * dt + 3 * g, 3)], homes[dt]) for dt in range(3)],
            sems.at[pl.ds(4 + 3 * g, 3)],
        )
    return small, copies


def start_weights(sources, outs, scratch):
    small, copies = name_weights(sources, outs, scratch)
    for copy in small + copies:
        copy.start()
    return small, copies


def finish_weights(small, copies, outs, scratch):
    u_ref, wi_ref, bi_ref, gain_ref, bm_ref = outs
    mid_ref, wi_raw, sems = scratch
    for copy in small:
        copy.wait()
    for dr in range(3):
        for dt in range(3):
            for dc in range(3):
                k = dt * 3 + dc
                at = (dr * 8 + k if k < 8 else 24 + dr) * Z
                wi_ref[at : at + Z] = wi_raw[9 * dt + 3 * dr + dc]
    for g in range(3):
        for copy in copies[3 * g : 3 * g + 3]:
            copy.wait()
        for tap in range(3 * g, 3 * g + 3):
            ends = 0.5 * (u_ref[0, tap].astype(jnp.float32) + u_ref[3, tap].astype(jnp.float32))
            mid = 0.5 * mid_ref[tap].astype(jnp.float32)
            u_ref[1, tap] = (ends + mid).astype(jnp.bfloat16)
            u_ref[2, tap] = (ends - mid).astype(jnp.bfloat16)


def join_kernel(*refs):
    rh_hbm, cw_hbm, got_ref, own_ref = refs[:4]
    sources, (ext_ref, size_ref), outs = refs[4:9], refs[9:11], refs[11:16]
    f32_ref, rh_ref, cw_ref, sems = refs[16:20]
    scratch = refs[20:]
    odd = lax.axis_index("tm") % 2 == 1

    @pl.when(odd)
    def _():
        start_weights(sources, outs, scratch)

    copies = fetch(((rh_hbm, rh_ref), (cw_hbm, cw_ref)), sems)
    i, j = lax.axis_index("ha"), lax.axis_index("wa")
    for copy in copies:
        copy.wait()
    h, w = rh_ref[i], cw_ref[j]
    up, down = jnp.maximum(i - 1, 0), jnp.minimum(i + 1, NH - 1)
    hu = rh_ref[up]
    lane = lanes_of()
    to_left, to_right = lane < 2, (lane >= w + 2) & (lane < w + 4)

    def strip(at, k, ok):
        return jnp.where(ok, got_ref[at, k * Z : (k + 1) * Z].astype(jnp.float32), 0.0)

    def sides(row):
        out = []
        for col, ok in ((jnp.maximum(j - 1, 0), j > 0), (jnp.minimum(j + 1, NW - 1), j < NW - 1)):
            row_ok = ok & (row >= 0) & (row < NH)
            out.append(strip(jnp.clip(row, 0, NH - 1) * NW + col, 0, row_ok))
        return out

    def put(at, base, pair, r):
        row = jnp.where(to_left, pltpu.roll(pair[0], (LANES - 2 * r) % LANES, 1), base)
        row = jnp.where(to_right, pltpu.roll(pair[1], (LANES + w + 2 - 2 * r) % LANES, 1), row)
        f32_ref[at] = row

    mid = sides(i)
    for r in range(TH):
        put(2 + r, own_ref[2 + r].astype(jnp.float32), mid, r)
    above, below = sides(i - 1), sides(i + 1)
    for k in range(2):
        put(k, strip(up * NW + j, k, i > 0), above, hu - 2 + k)
    for k in range(2):
        put(h + 2 + k, strip(down * NW + j, k, i < NH - 1), below, k)
    ext_ref[...] = f32_ref[...].astype(jnp.bfloat16)
    size_ref[0:8] = jnp.full((8, LANES), h, jnp.int32)
    size_ref[8:16] = jnp.full((8, LANES), w, jnp.int32)

    @pl.when(odd)
    def _():
        finish_weights(*name_weights(sources, outs, scratch), outs, scratch)


def weight_kernel(*refs):
    sources, outs, scratch = refs[:5], refs[10:15], refs[15:]

    @pl.when(lax.axis_index("tm") % 2 == 0)
    def _():
        finish_weights(*start_weights(sources, outs, scratch), outs, scratch)


def main_kernel(
    prev_ref, own_ref, size_ref, wi_ref, bi_ref, gain_ref, u_ref, bm_ref,
    out_ref, ta_ref, tb_ref, sa_ref, sb_ref, lhs_ref, short_ref, acc_ref,
):
    t, i, j = lax.axis_index("tm"), lax.axis_index("ha"), lax.axis_index("wa")
    h, w = size_ref[0:1, 0:1], size_ref[8:9, 0:1]
    lane = lax.broadcasted_iota(jnp.int32, (Z, LANES), 1)

    def taps(fields, r, turned, last):
        parts = []
        for field in fields:
            for dc in range(3):
                piece = field if dc == 0 else pltpu.roll(field, LANES - dc, 1)
                parts.append(piece.astype(jnp.bfloat16))
        turned[r] = jnp.concatenate(parts[:8], axis=0).T
        last[r * Z : (r + 1) * Z] = parts[8]

    for r in range(RE):
        prev, own = prev_ref[r].astype(jnp.float32), own_ref[r].astype(jnp.float32)
        one = jnp.where(lane < 3 * SPAN, pltpu.roll(prev, 3 * SPAN, 1), pltpu.roll(own, 3 * SPAN, 1))
        two = jnp.where(lane < 2 * SPAN, pltpu.roll(prev, 2 * SPAN, 1), pltpu.roll(own, 2 * SPAN, 1))
        taps((prev, one, two), r, ta_ref, sa_ref)
    for r in range(RE - 1):
        own = own_ref[r].astype(jnp.float32)
        nxt = own_ref[r + 1].astype(jnp.float32)
        fields = []
        for dt in range(3):
            a = own if dt == 0 else pltpu.roll(own, LANES - dt * SPAN, 1)
            b = nxt if dt == 2 else pltpu.roll(nxt, (2 - dt) * SPAN, 1)
            fields.append(jnp.where(lane < 2 * SPAN, a, b))
        taps(fields, r, tb_ref, sb_ref)

    bias, gain = bi_ref[...].reshape(1, C), gain_ref[...].reshape(1, C)
    pos = lax.broadcasted_iota(jnp.int32, (LANES, 1), 0)
    col = pos % SPAN
    col_ok = ((j > 0) | (col > 0)) & ((j < NW - 1) | (col <= w))
    early = (t > 0) | (pos >= 2 * SPAN)

    def row_ok(r):
        return ((i > 0) | (r > 0)) & ((i < NH - 1) | (r <= h))

    def entry_of(r):
        lhs = []
        for at, turned, last in ((r, ta_ref, sa_ref), (r + 1, ta_ref, sa_ref), (r, tb_ref, sb_ref)):
            rest = last[at * Z : (at + 3) * Z].T
            lhs.append(jnp.concatenate([turned[at], turned[at + 1], turned[at + 2], rest], axis=1))
        got = jnp.dot(jnp.concatenate(lhs, axis=0), wi_ref[...], preferred_element_type=jnp.float32)
        return (got + bias).astype(jnp.bfloat16).astype(jnp.float32)

    def active_of(entry, ok):
        meansq = jnp.mean(entry * entry, axis=-1, keepdims=True)
        v = entry * jnp.where(ok, lax.rsqrt(meansq + 1e-06), 0.0) * gain
        half = 0.5 * v
        return half + half * jnp.tanh(half)

    def step(q, _):
        r = 2 * q
        entry = entry_of(r)
        ok = jnp.concatenate(
            [
                col_ok & early & row_ok(r),
                col_ok & early & row_ok(r + 1),
                col_ok & ((row_ok(r) & (pos < 2 * SPAN)) | (row_ok(r + 1) & (pos >= 2 * SPAN))),
            ],
            axis=0,
        )
        active = active_of(entry, ok)
        ents = [entry[k * LANES : (k + 1) * LANES] for k in range(3)]
        acts = [active[k * LANES : (k + 1) * LANES] for k in range(3)]
        e, b = ents[2], acts[2]
        for k in range(2):
            frames = [acts[k][f * SPAN : (f + 1) * SPAN] for f in range(4)]
            frames += [b[(2 * k + f) * SPAN : (2 * k + f + 1) * SPAN] for f in range(2)]
            m = pl.multiple_of((r + k) * PR, 16)
            for p in range(4):
                pair = []
                for a in (frames[:4], frames[2:]):
                    pair.append((a[0] - a[2], a[1] + a[2], a[2] - a[1], a[1] - a[3])[p])
                for dc in range(3):
                    lhs_ref[p, pl.ds(m, PR), dc * C : (dc + 1) * C] = jnp.concatenate(
                        [v[dc : dc + TW] for v in pair], axis=0
                    ).astype(jnp.bfloat16)
            m = pl.multiple_of((r + k) * MR, 16)
            ef = [ents[k][(2 + f) * SPAN : (3 + f) * SPAN, :CO] for f in range(2)]
            ef += [e[(2 * k + f) * SPAN : (2 * k + f + 1) * SPAN, :CO] for f in range(2)]
            short_ref[pl.ds(m, MR), :] = jnp.concatenate([a[1 : 1 + TW] for a in ef], axis=0)
        return 0

    def mid(p, half):
        at = half * HALF * PR
        rows = jnp.concatenate(
            [lhs_ref[p, at + dr * PR : at + (dr + HALF) * PR] for dr in range(3)], axis=1
        )
        acc_ref[p, at : at + HALF * PR] = jnp.dot(
            rows, u_ref[p].reshape(9 * C, CO), preferred_element_type=jnp.float32
        )

    for q in range(HALF // 2 + 1):
        step(q, 0)
    for p in range(4):
        mid(p, 0)
        if HALF // 2 + 1 + p < RA // 2:
            step(HALF // 2 + 1 + p, 0)
    for p in range(4):
        mid(p, 1)

    bias_m = bm_ref[...].reshape(1, CO)
    keep_col = lax.broadcasted_iota(jnp.int32, (TW, 1), 0) < w
    for r in range(TH):
        ok = keep_col & (r < h)
        for pair in range(2):
            m = r * PR + pair * TW
            m0, m1, m2, m3 = (acc_ref[p, m : m + TW] for p in range(4))
            for f, mixed in ((2 * pair, m0 + m1 + m2), (2 * pair + 1, m1 - m2 - m3)):
                at = (r + 1) * MR + f * TW
                val = short_ref[at : at + TW] + mixed + bias_m
                out_ref[f, r] = jnp.where(ok, val, 0.0).astype(jnp.bfloat16)


def per_device(
    latents, in_weight, in_bias, norm_gain, mid_weight, mid_bias, row_heights, col_widths
):
    flipped = jnp.transpose(latents, (0, 1, 3, 2))
    vmem = pl.BlockSpec(memory_space=VM)
    hbm = pl.BlockSpec(memory_space=HBM)

    def stay(*arrays):
        return [pltpu.with_memory_space_constraint(a, HBM) for a in arrays]

    sizes_smem = [pltpu.SMEM((NH,), jnp.int32), pltpu.SMEM((NW,), jnp.int32)]
    bf16, f32 = jnp.bfloat16, jnp.float32
    limit = pltpu.CompilerParams(vmem_limit_bytes=4 * 1024 * 1024)
    blocks, own = pl.pallas_call(
        pack_kernel,
        out_shape=(VM((NH * NW, 2 * Z, LANES), bf16), VM((RE, Z, LANES), bf16)),
        in_specs=[hbm] * 3,
        out_specs=(vmem, vmem),
        scratch_shapes=[
            pltpu.VMEM((RE, Z, LANES), f32),
            pltpu.VMEM((F, TH, Z, TW), bf16),
            *sizes_smem,
            pltpu.SemaphoreType.DMA((3,)),
        ],
        compiler_params=limit,
    )(*stay(row_heights, col_widths, flipped))
    got = lax.all_to_all(blocks, ("ha", "wa"), 0, 0, tiled=True)
    params = stay(mid_weight, in_weight, in_bias, norm_gain, mid_bias)
    ready = (
        VM((4, 9, C, CO), bf16), VM((27 * Z, C), bf16), VM((C,), f32), VM((C,), f32), VM((CO,), f32)
    )
    rooms = [
        pltpu.VMEM((9, C, CO), bf16), pltpu.VMEM((27, Z, C), bf16), pltpu.SemaphoreType.DMA((13,))
    ]
    limit = pltpu.CompilerParams(vmem_limit_bytes=16 * 1024 * 1024)
    ext, sizes, *weights = pl.pallas_call(
        join_kernel,
        out_shape=(VM((RE, Z, LANES), bf16), VM((16, LANES), jnp.int32), *ready),
        in_specs=[hbm, hbm, vmem, vmem] + [hbm] * 5,
        out_specs=(vmem,) * 7,
        scratch_shapes=[
            pltpu.VMEM((RE, Z, LANES), f32), *sizes_smem, pltpu.SemaphoreType.DMA((2,)), *rooms
        ],
        compiler_params=limit,
    )(*stay(row_heights, col_widths), got, own, *params)
    groups = lax.axis_size("tm")
    prev = lax.ppermute(ext, "tm", [(g, g + 1) for g in range(groups - 1)])
    u, wi, bias, gain, bias_m = pl.pallas_call(
        weight_kernel,
        out_shape=ready,
        in_specs=[hbm] * 5 + [vmem] * 5,
        out_specs=(vmem,) * 5,
        scratch_shapes=rooms,
        input_output_aliases={5 + k: k for k in range(5)},
        compiler_params=limit,
        cost_estimate=pl.CostEstimate(flops=10_000_000, bytes_accessed=8_000_000, transcendentals=0),
    )(*params, *weights)
    return pl.pallas_call(
        main_kernel,
        out_shape=jax.ShapeDtypeStruct((F, TH, TW, CO), bf16),
        in_specs=[vmem] * 8,
        out_specs=vmem,
        scratch_shapes=[
            pltpu.VMEM((RE, LANES, LANES), bf16),
            pltpu.VMEM((RE, LANES, LANES), bf16),
            pltpu.VMEM((RE * Z, LANES), bf16),
            pltpu.VMEM((RE * Z, LANES), bf16),
            pltpu.VMEM((4, RA * PR, 3 * C), bf16),
            pltpu.VMEM((RA * MR, CO), f32),
            pltpu.VMEM((4, TH * PR, CO), f32),
        ],
        compiler_params=pltpu.CompilerParams(vmem_limit_bytes=32 * 1024 * 1024),
        cost_estimate=pl.CostEstimate(flops=4_500_000_000, bytes_accessed=8_000_000, transcendentals=1_000_000),
    )(prev, ext, sizes, wi, bias, gain, u, bias_m)


def solution(mesh):
    placed = (P("tm", "ha", "wa", None), P(), P(), P(), P(), P(), P(), P())
    return jax.shard_map(
        per_device, mesh=mesh, in_specs=placed, out_specs=P("tm", "ha", "wa", None), check_vma=False
    )
```

time: 49.1 us -> 33.5 us (0.68)
  the two profiles are of different devices: /device:TPU:225 before, /device:TPU:384 now
where the time goes in v2:
time: 33.5 us; the launch traced here: 33.3 us
  Pallas kernels  14.8 us (44%)
  blocking collectives  14.8 us (44%)
  starting transfers between devices  2.53 us (8%)
  waiting for transfers between devices  1.09 us (3%)
    all_to_all x1, blocking collectives, per_device(): got = lax.all_to_all(blocks, ('ha', 'wa'), 0, 0, tiled=True)  14.8 us
    pallas_call x1, Pallas kernels, per_device(): pl.pallas_call(main_kernel, out_shape=jax.ShapeDtypeStruct((F, TH, TW, CO...  9.51 us
    pallas_call x1, Pallas kernels, per_device(): pl.pallas_call(weight_kernel, out_shape=ready, in_specs=[hbm] * 5 + [vmem...  3.16 us
    ppermute x1, starting transfers between devices, per_device(): prev = lax.ppermute(ext, 'tm', [(g, g + 1) for g in range(groups - 1)])  2.53 us
    pallas_call x1, Pallas kernels, per_device(): pl.pallas_call(pack_kernel, out_shape=(VM((NH * NW, 2 * Z, LANES), bf16),...  1.18 us
    ppermute x1, waiting for transfers between devices, per_device(): prev = lax.ppermute(ext, 'tm', [(g, g + 1) for g in range(groups - 1)])  1.09 us
    pallas_call x1, Pallas kernels, per_device(): pl.pallas_call(join_kernel, out_shape=(VM((RE, Z, LANES), bf16), VM((16,...  0.96 us
  transfers between devices with their start and end apart: 1, of which 1 were waited for; matrix products, arithmetic and copies ran while one was open for 0% of the time, Pallas kernels for 9%

profile of v2, /device:TPU:384, one launch (start us, length us, event | category | flops | bytes accessed | tf_op | source)
XLA Modules:
  0.0 33.3 jit_solution(9127023115999315546)
XLA Ops:
  0.0 1.2 %shard_map.82 = (bf16[16,32,128]{2,1,0:T(8,128)(2,1)S(1)}, bf16[16,16,128]{2,1,0:T(8,128)(2,1)S(1)}) custom-call(s32[4]{0:T(128)} %refs_0_.2, s32[4]{0:T(128)} %refs_1_.2, bf16[4,12,16,24]{3,2,1,0:T(8,128)(2,1)} %bitcast.1), custom_call_target="tpu_custom_call" | custom-call | tf_op jit(solution)/shard_map/pallas_call | solution.py:320
  1.2 14.8 %all_to_all.5.refs_2_ = bf16[16,32,128]{2,1,0:T(8,128)(2,1)S(1)} all-to-all(bf16[16,32,128]{2,1,0:T(8,128)(2,1)S(1)} %get-tuple-element.19), channel_id=1, replica_groups=mesh['tm'=32,'ha'=4,'wa'=4] {'ha','wa'}, dimensions={0} | all-to-all | bytes 262144 | tf_op jit(solution)/shard_map/all_to_all | solution.py:333
  16.0 1.0 %shard_map.83 = (bf16[16,16,128]{2,1,0:T(8,128)(2,1)S(1)}, s32[16,128]{1,0:T(8,128)S(1)}, bf16[4,9,384,256]{3,2,1,0:T(8,128)(2,1)S(1)}, bf16[432,384]{1,0:T(8,12...) custom-call(s32[4]{0:T(128)} %refs_0_.2, s32[4]{0:T(128)} %refs_1_.2, ...), custom_call_target="tpu_custom_call" | custom-call | tf_op jit(solution)/shard_map/pallas_call | solution.py:342
  17.0 2.5 %collective-permute-start = (bf16[16,16,128]{2,1,0:T(8,128)(2,1)S(1)}, bf16[16,16,128]{2,1,0:T(8,128)(2,1)S(1)}, u32[]{:S(2)}, u32[]{:S(2)}) collective-permute-start(bf16[16,16,128]{2,1,0:T(8,128)(2,1)S(1)} %get-tuple-element.21.own_ref), channel_id=1, source_target_pairs={{0,16},{16,32},{32,48},{48,64},{64,80},{80,96},{96,112},{112,128},... | collective-permute-start | bytes 196616 | tf_op jit(solution)/shard_map/ppermute | solution.py:353
  19.5 3.2 %shard_map.84 = (bf16[4,9,384,256]{3,2,1,0:T(8,128)(2,1)S(1)}, bf16[432,384]{1,0:T(8,128)(2,1)S(1)}, f32[384]{0:T(512)S(1)}, f32[384]{0:T(512)S(1)}, f32[256]{0:T(256)S(1)}) custom-call(bf16[27,384,256]{2,1,0:T(8,128)(2,1)} %refs_0_.3, bf16[27,16,384]{2,1,0:T(8,128)(2,1)} %refs_1_.3, ...), custom_call_target="tpu_custom_call", output_to_operand_aliasing={{0}: (5, {}), {1}: (6, {}), {2}: (7, {}), {3}: (8, {}), {4}... | custom-call | flops 10000000 | bytes 8000000 | tf_op jit(solution)/shard_map/pallas_call | solution.py:354
  22.7 1.1 %collective-permute-done.prev_ref = bf16[16,16,128]{2,1,0:T(8,128)(2,1)S(1)} collective-permute-done((bf16[16,16,128]{2,1,0:T(8,128)(2,1)S(1)}, bf16[16,16,128]{2,1,0:T(8,128)(2,1)S(1)}, u32[]{:S(2)}, u32[]{:S(2)}) %collective-permute-start) | collective-permute-done | bytes 65568 | tf_op jit(solution)/shard_map/ppermute | solution.py:353
  23.8 9.5 %shard_map.85 = bf16[4,12,24,256]{3,2,1,0:T(8,128)(2,1)} custom-call(bf16[16,16,128]{2,1,0:T(8,128)(2,1)S(1)} %collective-permute-done.prev_ref, bf16[16,16,128]{2,1,0:T(8,128)(2,1)S(1)} %get-tuple-element.21.own_ref, s32[16,128]{1,0:T(8,128)S(1)} %get-tuple-element.22.size_ref, bf16[432,384]{1,0:T(8,128)(2,1)S(1)} %get-tuple-element.28.wi_ref, ...), custom_call_target="tpu_custom_call" | custom-call | flops 4499999744 | bytes 8000000 | tf_op jit(solution)/shard_map/pallas_call | solution.py:364
Async XLA Ops:
  17.0 6.8 %collective-permute-start = (bf16[16,16,128]{2,1,0:T(8,128)(2,1)S(1)}, bf16[16,16,128]{2,1,0:T(8,128)(2,1)S(1)}, u32[]{:S(2)}, u32[]{:S(2)}) collective-permute-start(bf16[16,16,128]{2,1,0:T(8,128)(2,1)S(1)} %get-tuple-element.21.own_ref), channel_id=1, source_target_pairs={{0,16},{16,32},{32,48},{48,64},{64,80},{80,96},{96,112},{112,128},... | collective-permute-start | bytes 196616 | tf_op jit(solution)/shard_map/ppermute | solution.py:353

commit v3 on v1

v3 whole, which is shorter than its diff:
```python
import jax
import jax.numpy as jnp
from jax import lax
from jax.experimental import pallas as pl
from jax.experimental.pallas import tpu as pltpu
from jax.sharding import PartitionSpec as P

F = 4
TH, TW = 12, 24
Z, C, CO = 16, 384, 256
NH, NW = 4, 4
LANES = 128
SPAN = 32
RE = TH + 4
RA = TH + 2
MR = F * TW
HALF = TH // 2
PR = 2 * TW

VM = pltpu.MemorySpace.VMEM
HBM = pltpu.MemorySpace.HBM


def lanes_of():
    return lax.broadcasted_iota(jnp.int32, (Z, LANES), 1) % SPAN


def name(pairs, sems):
    return [pltpu.make_async_copy(src, dst, sems.at[k]) for k, (src, dst) in enumerate(pairs)]


def fetch(pairs, sems):
    copies = name(pairs, sems)
    for copy in copies:
        copy.start()
    return copies


def pack_kernel(
    rh_hbm, cw_hbm, lat_hbm, blocks_ref, own_ref, size_ref, f32_ref, lat_ref, rh_ref, cw_ref, sems
):
    copies = fetch(((rh_hbm, rh_ref), (cw_hbm, cw_ref), (lat_hbm, lat_ref)), sems)
    i, j = lax.axis_index("ha"), lax.axis_index("wa")
    lane = lanes_of()
    blocks_ref[...] = jnp.zeros_like(blocks_ref)
    f32_ref[...] = jnp.zeros_like(f32_ref)
    for copy in copies:
        copy.wait()
    h, w = rh_ref[i], cw_ref[j]
    for k, size in enumerate((h, w, rh_ref[jnp.maximum(i - 1, 0)])):
        size_ref[8 * k : 8 * k + 8] = jnp.full((8, LANES), size, jnp.int32)
    for r in range(TH):
        for f in range(F):
            f32_ref[2 + r, :, f * SPAN + 2 : f * SPAN + 2 + TW] = lat_ref[f, r].astype(jnp.float32)
    right = jnp.zeros((Z, LANES), jnp.float32)
    left = jnp.zeros((Z, LANES), jnp.float32)
    for r in range(TH):
        row = f32_ref[2 + r]
        here = (lane // 2) == r
        right = jnp.where(here, pltpu.roll(row, (2 * r - w + LANES) % LANES, 1), right)
        left = jnp.where(here, pltpu.roll(row, (2 * r - 2) % LANES, 1), left)
    right = right.astype(jnp.bfloat16)
    left = left.astype(jnp.bfloat16)
    own_ref[...] = f32_ref[...].astype(jnp.bfloat16)
    for di in (-1, 0, 1):
        row_in = (i + di >= 0) & (i + di < NH)
        for dj, tile in ((-1, left), (1, right)):
            @pl.when(row_in & (j + dj >= 0) & (j + dj < NW))
            def _(di=di, dj=dj, tile=tile):
                blocks_ref[(i + di) * NW + j + dj, 0:Z] = tile

    @pl.when(i > 0)
    def _():
        for k in range(2):
            blocks_ref[(i - 1) * NW + j, k * Z : (k + 1) * Z] = f32_ref[2 + k].astype(jnp.bfloat16)

    @pl.when(i < NH - 1)
    def _():
        for k in range(2):
            blocks_ref[(i + 1) * NW + j, k * Z : (k + 1) * Z] = f32_ref[h + k].astype(jnp.bfloat16)


def turn_taps(fields, r, turned, last):
    parts = []
    for field in fields:
        for dc in range(3):
            piece = field if dc == 0 else pltpu.roll(field, LANES - dc, 1)
            parts.append(piece.astype(jnp.bfloat16))
    turned[r] = jnp.concatenate(parts[:8], axis=0).T
    last[r * Z : (r + 1) * Z] = parts[8]


def tap_rows(r, turned, last):
    rest = last[r * Z : (r + 3) * Z].T
    return jnp.concatenate([turned[r], turned[r + 1], turned[r + 2], rest], axis=1)


def entry_weights(wi_ref):
    order = [(dr, k) for dr in range(3) for k in range(8)] + [(dr, 8) for dr in range(3)]
    return jnp.concatenate([wi_ref[9 * (k // 3) + 3 * dr + k % 3] for dr, k in order], axis=0)


def entry_of(rows, wi, bias):
    got = jnp.dot(jnp.concatenate(rows, axis=0), wi, preferred_element_type=jnp.float32)
    return (got + bias).astype(jnp.bfloat16).astype(jnp.float32)


def active_of(entry, half_gain, ok):
    meansq = jnp.mean(entry * entry, axis=-1, keepdims=True)
    half = entry * jnp.where(ok, lax.rsqrt(meansq + 1e-06), 0.0) * half_gain
    return half + half * jnp.tanh(half)


def inside(size_ref):
    i, j = lax.axis_index("ha"), lax.axis_index("wa")
    h, w = size_ref[0:1, 0:1], size_ref[8:9, 0:1]
    pos = lax.broadcasted_iota(jnp.int32, (LANES, 1), 0)
    col = pos % SPAN
    col_ok = ((j > 0) | (col > 0)) & ((j < NW - 1) | (col <= w))

    def row_ok(r):
        return ((i > 0) | (r > 0)) & ((i < NH - 1) | (r <= h))

    return pos, col_ok, row_ok


def last_frames(own_ref, size_ref, wi_ref, bi_ref, gain_ref, act_ref, short_ref, turned, last):
    lane = lax.broadcasted_iota(jnp.int32, (Z, LANES), 1)
    for r in range(RE - 1):
        own = own_ref[r].astype(jnp.float32)
        nxt = own_ref[r + 1].astype(jnp.float32)
        fields = []
        for dt in range(3):
            a = own if dt == 0 else pltpu.roll(own, LANES - dt * SPAN, 1)
            b = nxt if dt == 2 else pltpu.roll(nxt, (2 - dt) * SPAN, 1)
            fields.append(jnp.where(lane < 2 * SPAN, a, b))
        turn_taps(fields, r, turned, last)
    wi = entry_weights(wi_ref)
    bias, half_gain = bi_ref[...].reshape(1, C), 0.5 * gain_ref[...].reshape(1, C)
    pos, col_ok, row_ok = inside(size_ref)
    steps = RA // 2
    for first, count in ((0, 4), (4, 3)):
        entry = entry_of([tap_rows(2 * q, turned, last) for q in range(first, first + count)], wi, bias)
        for q in range(first, first + count):
            e = entry[(q - first) * LANES : (q - first + 1) * LANES]
            r = 2 * q
            ok = col_ok & ((row_ok(r) & (pos < 2 * SPAN)) | (row_ok(r + 1) & (pos >= 2 * SPAN)))
            act_ref[q] = active_of(e, half_gain, ok)
            for k in range(2):
                short_ref[r + k] = jnp.concatenate(
                    [e[at + 1 : at + 1 + TW, :CO] for at in (2 * k * SPAN, (2 * k + 1) * SPAN)], axis=0
                )


def transform_weights(wm_ref, u_ref):
    for tap in range(9):
        ends = 0.5 * (wm_ref[tap].astype(jnp.float32) + wm_ref[18 + tap].astype(jnp.float32))
        mid = 0.5 * wm_ref[9 + tap].astype(jnp.float32)
        u_ref[0, tap] = (ends + mid).astype(jnp.bfloat16)
        u_ref[1, tap] = (ends - mid).astype(jnp.bfloat16)


def join_kernel(
    got_ref, own_ref, size_ref, wm_ref, ext_ref, u_ref, act_ref, short_ref, f32_ref,
):
    i, j = lax.axis_index("ha"), lax.axis_index("wa")
    h, w, hu = (jnp.max(size_ref[8 * k : 8 * k + 8].astype(jnp.float32)).astype(jnp.int32) for k in range(3))
    up, down = jnp.maximum(i - 1, 0), jnp.minimum(i + 1, NH - 1)
    lane = lanes_of()
    to_left, to_right = lane < 2, (lane >= w + 2) & (lane < w + 4)

    def strip(at, k, ok):
        return jnp.where(ok, got_ref[at, k * Z : (k + 1) * Z].astype(jnp.float32), 0.0)

    def sides(row):
        out = []
        for col, ok in ((jnp.maximum(j - 1, 0), j > 0), (jnp.minimum(j + 1, NW - 1), j < NW - 1)):
            row_ok = ok & (row >= 0) & (row < NH)
            out.append(strip(jnp.clip(row, 0, NH - 1) * NW + col, 0, row_ok))
        return out

    def put(at, base, pair, r):
        row = jnp.where(to_left, pltpu.roll(pair[0], (LANES - 2 * r) % LANES, 1), base)
        row = jnp.where(to_right, pltpu.roll(pair[1], (LANES + w + 2 - 2 * r) % LANES, 1), row)
        f32_ref[at] = row

    mid = sides(i)
    for r in range(TH):
        put(2 + r, own_ref[2 + r].astype(jnp.float32), mid, r)
    above, below = sides(i - 1), sides(i + 1)
    for k in range(2):
        put(k, strip(up * NW + j, k, i > 0), above, hu - 2 + k)
    for k in range(2):
        put(h + 2 + k, strip(down * NW + j, k, i < NH - 1), below, k)
    ext_ref[...] = f32_ref[...].astype(jnp.bfloat16)

    @pl.when(lax.axis_index("tm") % 2 == 1)
    def _():
        transform_weights(wm_ref, u_ref)


def ahead_kernel(
    wm_ref, wi_ref, bi_ref, gain_ref, own_ref, size_ref, u_in, act_in, short_in,
    u_ref, act_ref, short_ref, turned, last,
):
    @pl.when(lax.axis_index("tm") % 2 == 0)
    def _():
        transform_weights(wm_ref, u_ref)

    last_frames(own_ref, size_ref, wi_ref, bi_ref, gain_ref, act_ref, short_ref, turned, last)


def main_kernel(
    prev_ref, own_ref, size_ref, wi_ref, bi_ref, gain_ref, wm_ref, u_ref, act_ref, late_ref, bm_ref,
    out_ref, turned, last, lhs_ref, short_ref, acc_ref, made_ref, sems,
):
    lane = lax.broadcasted_iota(jnp.int32, (Z, LANES), 1)
    for r in range(RE):
        prev, own = prev_ref[r].astype(jnp.float32), own_ref[r].astype(jnp.float32)
        one = jnp.where(lane < 3 * SPAN, pltpu.roll(prev, 3 * SPAN, 1), pltpu.roll(own, 3 * SPAN, 1))
        two = jnp.where(lane < 2 * SPAN, pltpu.roll(prev, 2 * SPAN, 1), pltpu.roll(own, 2 * SPAN, 1))
        turn_taps((prev, one, two), r, turned, last)

    wi = entry_weights(wi_ref)
    bias, half_gain = bi_ref[...].reshape(1, C), 0.5 * gain_ref[...].reshape(1, C)
    w, h = size_ref[8:9, 0:1], size_ref[0:1, 0:1]
    pos, col_ok, row_ok = inside(size_ref)
    early = (lax.axis_index("tm") > 0) | (pos >= 2 * SPAN)

    def step(q):
        r = 2 * q
        entry = entry_of([tap_rows(r, turned, last), tap_rows(r + 1, turned, last)], wi, bias)
        yield
        ents = [entry[k * LANES : (k + 1) * LANES] for k in range(2)]
        acts = []
        for k in range(2):
            acts.append(active_of(ents[k], half_gain, col_ok & early & row_ok(r + k)))
            yield
        for k in range(2):
            frames = [acts[k][f * SPAN : (f + 1) * SPAN] for f in range(4)]
            frames += [act_ref[q, (2 * k + f) * SPAN : (2 * k + f + 1) * SPAN] for f in range(2)]
            m = (r + k) * PR
            for p in range(4):
                pair = []
                for a in (frames[:4], frames[2:]):
                    pair.append((a[0] - a[2], a[1] + a[2], a[2] - a[1], a[1] - a[3])[p])
                for dc in range(3):
                    lhs_ref[p, m : m + PR, dc * C : (dc + 1) * C] = jnp.concatenate(
                        [v[dc : dc + TW] for v in pair], axis=0
                    ).astype(jnp.bfloat16)
                if p % 2:
                    yield
            if 1 <= r + k <= TH:
                short_ref[r + k] = jnp.concatenate(
                    [ents[k][(2 + f) * SPAN + 1 : (2 + f) * SPAN + 1 + TW, :CO] for f in range(2)], axis=0
                )

    def plane(p):
        taps = (wm_ref[0:9], u_ref[0], u_ref[1], wm_ref[18:27])[p]
        return taps.reshape(9 * C, CO)

    def mid(p, first, rows):
        at = first * PR
        cuts = (0, 3456)
        for lo, hi in zip(cuts[:-1], cuts[1:]):
            parts = []
            for dr in range(3):
                a, b = max(lo - dr * 3 * C, 0), min(hi - dr * 3 * C, 3 * C)
                if a < b:
                    parts.append(lhs_ref[p, at + dr * PR : at + (dr + rows) * PR, a:b])
            got = jnp.dot(
                jnp.concatenate(parts, axis=1), plane(p)[lo:hi], preferred_element_type=jnp.float32
            )
            if lo == 0:
                acc_ref[p, at : at + rows * PR] = got
            else:
                acc_ref[p, at : at + rows * PR] += got
            yield

    def run(first, second, ratio):
        done = 0.0
        for _ in first:
            done += ratio
            while done >= 1.0:
                next(second, None)
                done -= 1.0
        for _ in second:
            pass

    def chain(parts):
        for part in parts:
            yield from part

    bias_m = bm_ref[...].reshape(1, CO)
    keep_col = lax.broadcasted_iota(jnp.int32, (TW, 1), 0) < w

    def write(half):
        for r in range(half * HALF, (half + 1) * HALF):
            ok = keep_col & (r < h)
            for pair in range(2):
                m = r * PR + pair * TW
                m0, m1, m2, m3 = (acc_ref[p, m : m + TW] for p in range(4))
                for f, mixed in ((2 * pair, m0 + m1 + m2), (2 * pair + 1, m1 - m2 - m3)):
                    short = (short_ref, late_ref)[pair][r + 1, (f % 2) * TW : (f % 2 + 1) * TW]
                    val = short + mixed + bias_m
                    made_ref[f, r] = jnp.where(ok, val, 0.0).astype(jnp.bfloat16)
            yield
        send(half).start()

    def send(half):
        part = pl.ds(half * HALF, HALF)
        return pltpu.make_async_copy(made_ref.at[:, part], out_ref.at[:, part], sems.at[half])

    for _ in chain(step(q) for q in range(4)):
        pass
    run(chain(mid(p, 0, HALF) for p in range(4)), chain(step(q) for q in range(4, 7)), 6.0)
    run(chain(mid(p, HALF, HALF) for p in range(4)), write(0), 2.0)
    for _ in write(1):
        pass
    send(0).wait()
    send(1).wait()


def per_device(
    latents, in_weight, in_bias, norm_gain, mid_weight, mid_bias, row_heights, col_widths
):
    flipped = jnp.transpose(latents, (0, 1, 3, 2))
    vmem = pl.BlockSpec(memory_space=VM)
    hbm = pl.BlockSpec(memory_space=HBM)

    def stay(*arrays):
        return [pltpu.with_memory_space_constraint(a, HBM) for a in arrays]

    bf16, f32 = jnp.bfloat16, jnp.float32
    limit = pltpu.CompilerParams(vmem_limit_bytes=4 * 1024 * 1024)
    blocks, own, sizes = pl.pallas_call(
        pack_kernel,
        out_shape=(
            VM((NH * NW, 2 * Z, LANES), bf16), VM((RE, Z, LANES), bf16), VM((24, LANES), jnp.int32)
        ),
        in_specs=[hbm] * 3,
        out_specs=(vmem,) * 3,
        scratch_shapes=[
            pltpu.VMEM((RE, Z, LANES), f32),
            pltpu.VMEM((F, TH, Z, TW), bf16),
            pltpu.SMEM((NH,), jnp.int32),
            pltpu.SMEM((NW,), jnp.int32),
            pltpu.SemaphoreType.DMA((3,)),
        ],
        compiler_params=limit,
        cost_estimate=pl.CostEstimate(flops=10_000_000_000, bytes_accessed=20_000_000, transcendentals=0),
    )(*stay(row_heights, col_widths, flipped))
    got = lax.all_to_all(blocks, ("ha", "wa"), 0, 0, tiled=True)
    ahead = (VM((2, 9, C, CO), bf16), VM((RA // 2, LANES, C), f32), VM((RA, PR, CO), f32))
    turned = [pltpu.VMEM((RE, LANES, LANES), bf16), pltpu.VMEM((RE * Z, LANES), bf16)]
    entry_params = (in_weight, in_bias, norm_gain)
    ext, *made = pl.pallas_call(
        join_kernel,
        out_shape=(VM((RE, Z, LANES), bf16), *ahead),
        in_specs=[vmem] * 4,
        out_specs=(vmem,) * 4,
        scratch_shapes=[pltpu.VMEM((RE, Z, LANES), f32)],
        compiler_params=limit,
    )(got, own, sizes, mid_weight)
    groups = lax.axis_size("tm")
    prev = lax.ppermute(ext, "tm", [(g, g + 1) for g in range(groups - 1)])
    made = pl.pallas_call(
        ahead_kernel,
        out_shape=ahead,
        in_specs=[vmem] * 9,
        out_specs=(vmem,) * 3,
        scratch_shapes=turned,
        input_output_aliases={6: 0, 7: 1, 8: 2},
        compiler_params=limit,
        cost_estimate=pl.CostEstimate(flops=400_000_000, bytes_accessed=8_000_000, transcendentals=400_000),
    )(mid_weight, *entry_params, ext, sizes, *made)
    return pl.pallas_call(
        main_kernel,
        out_shape=jax.ShapeDtypeStruct((F, TH, TW, CO), bf16),
        in_specs=[vmem] * 11,
        out_specs=hbm,
        scratch_shapes=[
            *turned,
            pltpu.VMEM((4, RA * PR, 3 * C), bf16),
            pltpu.VMEM((RA, PR, CO), f32),
            pltpu.VMEM((4, TH * PR, CO), f32),
            pltpu.VMEM((F, TH, TW, CO), bf16),
            pltpu.SemaphoreType.DMA((2,)),
        ],
        compiler_params=pltpu.CompilerParams(vmem_limit_bytes=32 * 1024 * 1024),
        cost_estimate=pl.CostEstimate(flops=4_500_000_000, bytes_accessed=8_000_000, transcendentals=1_000_000),
    )(prev, ext, sizes, *entry_params, mid_weight, *made, mid_bias)


def solution(mesh):
    placed = (P("tm", "ha", "wa", None), P(), P(), P(), P(), P(), P(), P())
    return jax.shard_map(
        per_device, mesh=mesh, in_specs=placed, out_specs=P("tm", "ha", "wa", None), check_vma=False
    )
```

time: 49.1 us -> 32.5 us (0.66)
  local copies, waits for them, and re-layouts: 7.7 us -> 0.03 us
  Pallas kernels: 20.5 us -> 13.1 us
  starting transfers between devices: 6.71 us -> 5.57 us
    pallas_call x1, Pallas kernels: 17 us -> 8.55 us  [per_device(): pl.pallas_call(main_kernel, out_shape=jax.ShapeDtypeStruct((F, TH, TW, CO...]
    unnamed x10 -> x12, local copies, waits for them, and re-layouts: 5.33 us -> 0.03 us
    reshape x3 -> x0, local copies, waits for them, and re-layouts: 2.38 us -> none  [the longest x1 1.01 us: per_device(): in_weight.reshape(3, 3, 3, Z, C).transpose(1, 0, 2, 3, 4).reshape(27 * Z, C)]
    ppermute x1, starting transfers between devices: 6.71 us -> 5.57 us  [per_device(): prev = lax.ppermute(ext, 'tm', [(g, g + 1) for g in range(groups - 1)])]
    pallas_call x2 -> x3, Pallas kernels: 3.5 us -> 4.58 us  [the longest x1 1.84 us: per_device(): pl.pallas_call(ahead_kernel, out_shape=ahead, in_specs=[vmem] * 9, out_sp...]
  transfers between devices with their start and end apart: 1 -> 1, of which waited for: 0 -> 0; matrix products, arithmetic and copies ran while one was open for 5% -> 0% of each run, Pallas kernels for 0% -> 6%
where the time goes in v3:
time: 32.5 us; the launch traced here: 32.4 us
  blocking collectives  13.6 us (42%)
  Pallas kernels  13.1 us (40%)
  starting transfers between devices  5.57 us (17%)
    all_to_all x1, blocking collectives, per_device(): got = lax.all_to_all(blocks, ('ha', 'wa'), 0, 0, tiled=True)  13.6 us
    pallas_call x1, Pallas kernels, per_device(): pl.pallas_call(main_kernel, out_shape=jax.ShapeDtypeStruct((F, TH, TW, CO...  8.55 us
    ppermute x1, starting transfers between devices, per_device(): prev = lax.ppermute(ext, 'tm', [(g, g + 1) for g in range(groups - 1)])  5.57 us
    pallas_call x1, Pallas kernels, per_device(): pl.pallas_call(ahead_kernel, out_shape=ahead, in_specs=[vmem] * 9, out_sp...  1.84 us
    pallas_call x1, Pallas kernels, per_device(): pl.pallas_call(join_kernel, out_shape=(VM((RE, Z, LANES), bf16), *ahead),...  1.4 us
    pallas_call x1, Pallas kernels, per_device(): pl.pallas_call(pack_kernel, out_shape=(VM((NH * NW, 2 * Z, LANES), bf16),...  1.33 us
  transfers between devices with their start and end apart: 1, of which 0 were waited for; matrix products, arithmetic and copies ran while one was open for 0% of the time, Pallas kernels for 6%

profile of v3, /device:TPU:225, one launch (start us, length us, event | category | flops | bytes accessed | tf_op | source)
XLA Modules:
  0.0 32.4 jit_solution(16731197522395012254)
XLA Ops:
  0.0 0.0 slice-start
  0.0 0.0 slice-start.1
  0.0 1.3 %shard_map.82 = (bf16[16,32,128]{2,1,0:T(8,128)(2,1)S(1)}, bf16[16,16,128]{2,1,0:T(8,128)(2,1)S(1)}, s32[24,128]{1,0:T(8,128)S(1)}) custom-call(s32[4]{0:T(128)} %rh_hbm.1, s32[4]{0:T(128)} %cw_hbm.1, bf16[4,12,16,24]{3,2,1,0:T(8,128)(2,1)} %bitcast.3), custom_call_target="tpu_custom_call" | custom-call | flops 10000000000 | bytes 20000000 | tf_op jit(solution)/shard_map/pallas_call | solution.py:336
  1.3 0.0 copy-start
  1.4 0.0 copy-start.1
  1.4 0.0 copy-start.2
  1.4 13.6 %all_to_all.5.got_ref = bf16[16,32,128]{2,1,0:T(8,128)(2,1)S(1)} all-to-all(bf16[16,32,128]{2,1,0:T(8,128)(2,1)S(1)} %get-tuple-element.15), channel_id=1, replica_groups=mesh['tm'=32,'ha'=4,'wa'=4] {'ha','wa'}, dimensions={0} | all-to-all | bytes 262144 | tf_op jit(solution)/shard_map/all_to_all | solution.py:353
  14.9 0.0 slice-done
  14.9 0.0 slice-done.1
  14.9 1.4 %shard_map.83 = (bf16[16,16,128]{2,1,0:T(8,128)(2,1)S(1)}, bf16[2,9,384,256]{3,2,1,0:T(8,128)(2,1)S(1)}, f32[7,128,384]{2,1,0:T(8,128)S(1)}, f32[14,48,256]{2,1,0:T(8,128)S(1)}) custom-call(bf16[16,32,128]{2,1,0:T(8,128)(2,1)S(1)} %all_to_all.5.got_ref, bf16[16,16,128]{2,1,0:T(8,128)(2,1)S(1)} %get-tuple-element.16.own_ref, ...), custom_call_target="tpu_custom_call" | custom-call | tf_op jit(solution)/shard_map/pallas_call | solution.py:357
  16.3 5.6 %collective-permute-start = (bf16[16,16,128]{2,1,0:T(8,128)(2,1)S(1)}, bf16[16,16,128]{2,1,0:T(8,128)(2,1)S(1)}, u32[]{:S(2)}, u32[]{:S(2)}) collective-permute-start(bf16[16,16,128]{2,1,0:T(8,128)(2,1)S(1)} %get-tuple-element.18.own_ref), channel_id=1, source_target_pairs={{0,16},{16,32},{32,48},{48,64},{64,80},{80,96},{96,112},{112,128},... | collective-permute-start | bytes 196616 | tf_op jit(solution)/shard_map/ppermute | solution.py:366
  21.9 0.0 copy-done
  21.9 0.0 copy-done.1
  21.9 0.0 copy-done.2
  22.0 0.0 copy-start.3
  22.0 1.8 %shard_map.84 = (bf16[2,9,384,256]{3,2,1,0:T(8,128)(2,1)S(1)}, f32[7,128,384]{2,1,0:T(8,128)S(1)}, f32[14,48,256]{2,1,0:T(8,128)S(1)}) custom-call(bf16[27,384,256]{2,1,0:T(8,128)(2,1)S(1)} %bitcast.2, bf16[27,16,384]{2,1,0:T(8,128)(2,1)S(1)} %copy-done, f32[384]{0:T(512)S(1)} %copy-done.1, ...), custom_call_target="tpu_custom_call", output_to_operand_aliasing={{0}: (6, {}), {1}: (7, {}), {2}: (8, {})} | custom-call | flops 400000000 | bytes 8000000 | tf_op jit(solution)/shard_map/pallas_call | solution.py:367
  23.8 0.0 collective-permute-done.prev_ref
  23.8 0.0 copy-done.3
  23.8 8.5 %shard_map.85 = bf16[4,12,24,256]{3,2,1,0:T(8,128)(2,1)} custom-call(bf16[16,16,128]{2,1,0:T(8,128)(2,1)S(1)} %collective-permute-done.prev_ref, bf16[16,16,128]{2,1,0:T(8,128)(2,1)S(1)} %get-tuple-element.18.own_ref, s32[24,128]{1,0:T(8,128)S(1)} %get-tuple-element.17.size_ref, bf16[27,16,384]{2,1,0:T(8,128)(2,1)S(1)} %copy-done, f32[384]{0:T(512)S(1)} %copy-done.1, ...), custom_call_target="tpu_custom_call" | custom-call | flops 4499999744 | bytes 8000000 | tf_op jit(solution)/shard_map/pallas_call | solution.py:377
  (1 shorter events, 0.0 us)
Async XLA Ops:
  0.0 14.9 %slice-start = ((s8[5308416]{0:T(1024)(128)(4,1)}), s8[4194304]{0:T(1024)(128)(4,1)S(1)}, s32[]{:S(2)}) async-start(s8[5308416]{0:T(1024)(128)(4,1)} %bitcast.1), calls=%async_computation.1 | async-start | bytes 8388608
  0.0 14.9 %slice-start.1 = ((s8[5308416]{0:T(1024)(128)(4,1)}), s8[1114112]{0:T(1024)(128)(4,1)S(1)}, s32[]{:S(2)}) async-start(s8[5308416]{0:T(1024)(128)(4,1)} %bitcast.1), calls=%async_computation.2 | async-start | bytes 2228224
  1.3 20.6 %copy-start = (bf16[27,16,384]{2,1,0:T(8,128)(2,1)S(1)}, bf16[27,16,384]{2,1,0:T(8,128)(2,1)}, u32[]{:S(2)}) copy-start(bf16[27,16,384]{2,1,0:T(8,128)(2,1)} %wi_ref.3) | copy-start | bytes 995332
  1.4 20.6 %copy-start.1 = (f32[384]{0:T(512)S(1)}, f32[384]{0:T(512)}, u32[]{:S(2)}) copy-start(f32[384]{0:T(512)} %bi_ref.3) | copy-start | bytes 4612
  1.4 20.6 %copy-start.2 = (f32[384]{0:T(512)S(1)}, f32[384]{0:T(512)}, u32[]{:S(2)}) copy-start(f32[384]{0:T(512)} %gain_ref.3) | copy-start | bytes 4612
  16.3 7.5 %collective-permute-start = (bf16[16,16,128]{2,1,0:T(8,128)(2,1)S(1)}, bf16[16,16,128]{2,1,0:T(8,128)(2,1)S(1)}, u32[]{:S(2)}, u32[]{:S(2)}) collective-permute-start(bf16[16,16,128]{2,1,0:T(8,128)(2,1)S(1)} %get-tuple-element.18.own_ref), channel_id=1, source_target_pairs={{0,16},{16,32},{32,48},{48,64},{64,80},{80,96},{96,112},{112,128},... | collective-permute-start | bytes 196616 | tf_op jit(solution)/shard_map/ppermute | solution.py:366
  22.0 1.9 %copy-start.3 = (f32[256]{0:T(256)S(1)}, f32[256]{0:T(256)}, u32[]{:S(2)}) copy-start(f32[256]{0:T(256)} %bm_ref.1) | copy-start | bytes 3076

commit v4 on v3

--- a/solution.py
+++ b/solution.py
@@ -124,9 +124,12 @@
     return pos, col_ok, row_ok
 
 
-def last_frames(own_ref, size_ref, wi_ref, bi_ref, gain_ref, act_ref, short_ref, turned, last):
+PARTS = ((0, 4), (4, 3))
+
+
+def last_frames(own_ref, size_ref, wi_ref, bi_ref, gain_ref, act_ref, short_ref, turned, last, parts):
     lane = lax.broadcasted_iota(jnp.int32, (Z, LANES), 1)
-    for r in range(RE - 1):
+    for r in range(2 * parts[0][0], 2 * sum(parts[-1]) + 1):
         own = own_ref[r].astype(jnp.float32)
         nxt = own_ref[r + 1].astype(jnp.float32)
         fields = []
@@ -138,8 +141,7 @@
     wi = entry_weights(wi_ref)
     bias, half_gain = bi_ref[...].reshape(1, C), 0.5 * gain_ref[...].reshape(1, C)
     pos, col_ok, row_ok = inside(size_ref)
-    steps = RA // 2
-    for first, count in ((0, 4), (4, 3)):
+    for first, count in parts:
         entry = entry_of([tap_rows(2 * q, turned, last) for q in range(first, first + count)], wi, bias)
         for q in range(first, first + count):
             e = entry[(q - first) * LANES : (q - first + 1) * LANES]
@@ -154,14 +156,15 @@
 
 def transform_weights(wm_ref, u_ref):
     for tap in range(9):
-        ends = 0.5 * (wm_ref[tap].astype(jnp.float32) + wm_ref[18 + tap].astype(jnp.float32))
-        mid = 0.5 * wm_ref[9 + tap].astype(jnp.float32)
+        ends = wm_ref[tap].astype(jnp.float32) + wm_ref[18 + tap].astype(jnp.float32)
+        mid = wm_ref[9 + tap].astype(jnp.float32)
         u_ref[0, tap] = (ends + mid).astype(jnp.bfloat16)
         u_ref[1, tap] = (ends - mid).astype(jnp.bfloat16)
 
 
 def join_kernel(
-    got_ref, own_ref, size_ref, wm_ref, ext_ref, u_ref, act_ref, short_ref, f32_ref,
+    got_ref, own_ref, size_ref, wm_ref, wi_ref, bi_ref, gain_ref,
+    ext_ref, u_ref, act_ref, short_ref, f32_ref, turned, last,
 ):
     i, j = lax.axis_index("ha"), lax.axis_index("wa")
     h, w, hu = (jnp.max(size_ref[8 * k : 8 * k + 8].astype(jnp.float32)).astype(jnp.int32) for k in range(3))
@@ -197,6 +200,9 @@
     @pl.when(lax.axis_index("tm") % 2 == 1)
     def _():
         transform_weights(wm_ref, u_ref)
+        last_frames(
+            ext_ref, size_ref, wi_ref, bi_ref, gain_ref, act_ref, short_ref, turned, last, PARTS[:1]
+        )
 
 
 def ahead_kernel(
@@ -206,8 +212,15 @@
     @pl.when(lax.axis_index("tm") % 2 == 0)
     def _():
         transform_weights(wm_ref, u_ref)
-
-    last_frames(own_ref, size_ref, wi_ref, bi_ref, gain_ref, act_ref, short_ref, turned, last)
+        last_frames(
+            own_ref, size_ref, wi_ref, bi_ref, gain_ref, act_ref, short_ref, turned, last, PARTS
+        )
+
+    @pl.when(lax.axis_index("tm") % 2 == 1)
+    def _():
+        last_frames(
+            own_ref, size_ref, wi_ref, bi_ref, gain_ref, act_ref, short_ref, turned, last, PARTS[1:]
+        )
 
 
 def main_kernel(
@@ -300,7 +313,7 @@
             for pair in range(2):
                 m = r * PR + pair * TW
                 m0, m1, m2, m3 = (acc_ref[p, m : m + TW] for p in range(4))
-                for f, mixed in ((2 * pair, m0 + m1 + m2), (2 * pair + 1, m1 - m2 - m3)):
+                for f, mixed in ((2 * pair, m0 + 0.5 * (m1 + m2)), (2 * pair + 1, 0.5 * (m1 - m2) - m3)):
                     short = (short_ref, late_ref)[pair][r + 1, (f % 2) * TW : (f % 2 + 1) * TW]
                     val = short + mixed + bias_m
                     made_ref[f, r] = jnp.where(ok, val, 0.0).astype(jnp.bfloat16)
@@ -357,11 +370,11 @@
     ext, *made = pl.pallas_call(
         join_kernel,
         out_shape=(VM((RE, Z, LANES), bf16), *ahead),
-        in_specs=[vmem] * 4,
+        in_specs=[vmem] * 7,
         out_specs=(vmem,) * 4,
-        scratch_shapes=[pltpu.VMEM((RE, Z, LANES), f32)],
+        scratch_shapes=[pltpu.VMEM((RE, Z, LANES), f32), *turned],
         compiler_params=limit,
-    )(got, own, sizes, mid_weight)
+    )(got, own, sizes, mid_weight, *entry_params)
     groups = lax.axis_size("tm")
     prev = lax.ppermute(ext, "tm", [(g, g + 1) for g in range(groups - 1)])
     made = pl.pallas_call(

time: 32.5 us -> 32.3 us (level)
  the two profiles are of different devices: /device:TPU:225 before, /device:TPU:256 now
where the time goes in v4:
time: 32.3 us; the launch traced here: 32.1 us
  blocking collectives  15 us (46%)
  Pallas kernels  13.5 us (42%)
  starting transfers between devices  2.9 us (9%)
  waiting for transfers between devices  0.46 us (1%)
    all_to_all x1, blocking collectives, per_device(): got = lax.all_to_all(blocks, ('ha', 'wa'), 0, 0, tiled=True)  15 us
    pallas_call x1, Pallas kernels, per_device(): pl.pallas_call(main_kernel, out_shape=jax.ShapeDtypeStruct((F, TH, TW, CO...  8.54 us
    pallas_call x1, Pallas kernels, per_device(): pl.pallas_call(ahead_kernel, out_shape=ahead, in_specs=[vmem] * 9, out_sp...  3.41 us
    ppermute x1, starting transfers between devices, per_device(): prev = lax.ppermute(ext, 'tm', [(g, g + 1) for g in range(groups - 1)])  2.9 us
    pallas_call x1, Pallas kernels, per_device(): pl.pallas_call(pack_kernel, out_shape=(VM((NH * NW, 2 * Z, LANES), bf16),...  1.34 us
  transfers between devices with their start and end apart: 1, of which 1 were waited for; matrix products, arithmetic and copies ran while one was open for 0% of the time, Pallas kernels for 11%

profile of v4, /device:TPU:256, one launch (start us, length us, event | category | flops | bytes accessed | tf_op | source)
XLA Modules:
  0.0 32.1 jit_solution(8279607940022555052)
XLA Ops:
  0.0 0.0 slice-start
  0.0 0.0 slice-start.1
  0.0 0.0 copy-start
  0.0 0.0 copy-start.1
  0.0 0.0 copy-start.2
  0.0 1.3 %shard_map.82 = (bf16[16,32,128]{2,1,0:T(8,128)(2,1)S(1)}, bf16[16,16,128]{2,1,0:T(8,128)(2,1)S(1)}, s32[24,128]{1,0:T(8,128)S(1)}) custom-call(s32[4]{0:T(128)} %rh_hbm.1, s32[4]{0:T(128)} %cw_hbm.1, bf16[4,12,16,24]{3,2,1,0:T(8,128)(2,1)} %bitcast.3), custom_call_target="tpu_custom_call" | custom-call | flops 10000000000 | bytes 20000000 | tf_op jit(solution)/shard_map/pallas_call | solution.py:349
  1.4 15.0 %all_to_all.5.got_ref = bf16[16,32,128]{2,1,0:T(8,128)(2,1)S(1)} all-to-all(bf16[16,32,128]{2,1,0:T(8,128)(2,1)S(1)} %get-tuple-element.15), channel_id=1, replica_groups=mesh['tm'=32,'ha'=4,'wa'=4] {'ha','wa'}, dimensions={0} | all-to-all | bytes 262144 | tf_op jit(solution)/shard_map/all_to_all | solution.py:366
  16.3 0.0 slice-done
  16.3 0.0 slice-done.1
  16.3 0.0 copy-done
  16.3 0.0 copy-done.1
  16.4 0.0 copy-done.2
  16.4 0.3 shard_map.83
  16.6 2.9 %collective-permute-start = (bf16[16,16,128]{2,1,0:T(8,128)(2,1)S(1)}, bf16[16,16,128]{2,1,0:T(8,128)(2,1)S(1)}, u32[]{:S(2)}, u32[]{:S(2)}) collective-permute-start(bf16[16,16,128]{2,1,0:T(8,128)(2,1)S(1)} %get-tuple-element.18.own_ref), channel_id=1, source_target_pairs={{0,16},{16,32},{32,48},{48,64},{64,80},{80,96},{96,112},{112,128},... | collective-permute-start | bytes 196616 | tf_op jit(solution)/shard_map/ppermute | solution.py:379
  19.5 0.0 copy-start.3
  19.5 3.4 %shard_map.84 = (bf16[2,9,384,256]{3,2,1,0:T(8,128)(2,1)S(1)}, f32[7,128,384]{2,1,0:T(8,128)S(1)}, f32[14,48,256]{2,1,0:T(8,128)S(1)}) custom-call(bf16[27,384,256]{2,1,0:T(8,128)(2,1)S(1)} %bitcast.2, bf16[27,16,384]{2,1,0:T(8,128)(2,1)S(1)} %copy-done, f32[384]{0:T(512)S(1)} %copy-done.1, ...), custom_call_target="tpu_custom_call", output_to_operand_aliasing={{0}: (6, {}), {1}: (7, {}), {2}: (8, {})} | custom-call | flops 400000000 | bytes 8000000 | tf_op jit(solution)/shard_map/pallas_call | solution.py:380
  23.0 0.5 %collective-permute-done.prev_ref = bf16[16,16,128]{2,1,0:T(8,128)(2,1)S(1)} collective-permute-done((bf16[16,16,128]{2,1,0:T(8,128)(2,1)S(1)}, bf16[16,16,128]{2,1,0:T(8,128)(2,1)S(1)}, u32[]{:S(2)}, u32[]{:S(2)}) %collective-permute-start) | collective-permute-done | bytes 65568 | tf_op jit(solution)/shard_map/ppermute | solution.py:379
  23.4 0.0 copy-done.3
  23.4 8.5 %shard_map.85 = bf16[4,12,24,256]{3,2,1,0:T(8,128)(2,1)} custom-call(bf16[16,16,128]{2,1,0:T(8,128)(2,1)S(1)} %collective-permute-done.prev_ref, bf16[16,16,128]{2,1,0:T(8,128)(2,1)S(1)} %get-tuple-element.18.own_ref, s32[24,128]{1,0:T(8,128)S(1)} %get-tuple-element.17.size_ref, bf16[27,16,384]{2,1,0:T(8,128)(2,1)S(1)} %copy-done, f32[384]{0:T(512)S(1)} %copy-done.1, ...), custom_call_target="tpu_custom_call" | custom-call | flops 4499999744 | bytes 8000000 | tf_op jit(solution)/shard_map/pallas_call | solution.py:390
  (1 shorter events, 0.0 us)
Async XLA Ops:
  0.0 16.3 %slice-start = ((s8[5308416]{0:T(1024)(128)(4,1)}), s8[4194304]{0:T(1024)(128)(4,1)S(1)}, s32[]{:S(2)}) async-start(s8[5308416]{0:T(1024)(128)(4,1)} %bitcast.1), calls=%async_computation.1 | async-start | bytes 8388608
  0.0 16.3 %slice-start.1 = ((s8[5308416]{0:T(1024)(128)(4,1)}), s8[1114112]{0:T(1024)(128)(4,1)S(1)}, s32[]{:S(2)}) async-start(s8[5308416]{0:T(1024)(128)(4,1)} %bitcast.1), calls=%async_computation.2 | async-start | bytes 2228224
  0.0 16.3 %copy-start = (bf16[27,16,384]{2,1,0:T(8,128)(2,1)S(1)}, bf16[27,16,384]{2,1,0:T(8,128)(2,1)}, u32[]{:S(2)}) copy-start(bf16[27,16,384]{2,1,0:T(8,128)(2,1)} %wi_ref.5) | copy-start | bytes 995332
  0.0 16.3 %copy-start.1 = (f32[384]{0:T(512)S(1)}, f32[384]{0:T(512)}, u32[]{:S(2)}) copy-start(f32[384]{0:T(512)} %bi_ref.5) | copy-start | bytes 4612
  0.0 16.3 %copy-start.2 = (f32[384]{0:T(512)S(1)}, f32[384]{0:T(512)}, u32[]{:S(2)}) copy-start(f32[384]{0:T(512)} %gain_ref.5) | copy-start | bytes 4612
  16.6 6.8 %collective-permute-start = (bf16[16,16,128]{2,1,0:T(8,128)(2,1)S(1)}, bf16[16,16,128]{2,1,0:T(8,128)(2,1)S(1)}, u32[]{:S(2)}, u32[]{:S(2)}) collective-permute-start(bf16[16,16,128]{2,1,0:T(8,128)(2,1)S(1)} %get-tuple-element.18.own_ref), channel_id=1, source_target_pairs={{0,16},{16,32},{32,48},{48,64},{64,80},{80,96},{96,112},{112,128},... | collective-permute-start | bytes 196616 | tf_op jit(solution)/shard_map/ppermute | solution.py:379
  19.5 3.9 %copy-start.3 = (f32[256]{0:T(256)S(1)}, f32[256]{0:T(256)}, u32[]{:S(2)}) copy-start(f32[256]{0:T(256)} %bm_ref.1) | copy-start | bytes 3076

commit v5 on v4

--- a/solution.py
+++ b/solution.py
@@ -326,7 +326,7 @@
 
     for _ in chain(step(q) for q in range(4)):
         pass
-    run(chain(mid(p, 0, HALF) for p in range(4)), chain(step(q) for q in range(4, 7)), 6.0)
+    run(chain(mid(p, 0, HALF) for p in range(4)), chain(step(q) for q in range(4, 7)), 4.0)
     run(chain(mid(p, HALF, HALF) for p in range(4)), write(0), 2.0)
     for _ in write(1):
         pass

time: 32.3 us -> 32.2 us (level)
  the two profiles are of different devices: /device:TPU:256 before, /device:TPU:384 now
where the time goes in v5:
time: 32.2 us; the launch traced here: 32 us
  blocking collectives  15 us (47%)
  Pallas kernels  13.4 us (42%)
  starting transfers between devices  2.89 us (9%)
  waiting for transfers between devices  0.46 us (1%)
    all_to_all x1, blocking collectives, per_device(): got = lax.all_to_all(blocks, ('ha', 'wa'), 0, 0, tiled=True)  15 us
    pallas_call x1, Pallas kernels, per_device(): pl.pallas_call(main_kernel, out_shape=jax.ShapeDtypeStruct((F, TH, TW, CO...  8.44 us
    pallas_call x1, Pallas kernels, per_device(): pl.pallas_call(ahead_kernel, out_shape=ahead, in_specs=[vmem] * 9, out_sp...  3.41 us
    ppermute x1, starting transfers between devices, per_device(): prev = lax.ppermute(ext, 'tm', [(g, g + 1) for g in range(groups - 1)])  2.89 us
    pallas_call x1, Pallas kernels, per_device(): pl.pallas_call(pack_kernel, out_shape=(VM((NH * NW, 2 * Z, LANES), bf16),...  1.34 us
  transfers between devices with their start and end apart: 1, of which 1 were waited for; matrix products, arithmetic and copies ran while one was open for 0% of the time, Pallas kernels for 11%

profile of v5, /device:TPU:384, one launch (start us, length us, event | category | flops | bytes accessed | tf_op | source)
XLA Modules:
  0.0 32.0 jit_solution(9872495107235431974)
XLA Ops:
  0.0 0.0 slice-start
  0.0 0.0 slice-start.1
  0.0 0.0 copy-start
  0.0 0.0 copy-start.1
  0.0 0.0 copy-start.2
  0.0 1.3 %shard_map.82 = (bf16[16,32,128]{2,1,0:T(8,128)(2,1)S(1)}, bf16[16,16,128]{2,1,0:T(8,128)(2,1)S(1)}, s32[24,128]{1,0:T(8,128)S(1)}) custom-call(s32[4]{0:T(128)} %rh_hbm.1, s32[4]{0:T(128)} %cw_hbm.1, bf16[4,12,16,24]{3,2,1,0:T(8,128)(2,1)} %bitcast.3), custom_call_target="tpu_custom_call" | custom-call | flops 10000000000 | bytes 20000000 | tf_op jit(solution)/shard_map/pallas_call | solution.py:349
  1.4 15.0 %all_to_all.5.got_ref = bf16[16,32,128]{2,1,0:T(8,128)(2,1)S(1)} all-to-all(bf16[16,32,128]{2,1,0:T(8,128)(2,1)S(1)} %get-tuple-element.15), channel_id=1, replica_groups=mesh['tm'=32,'ha'=4,'wa'=4] {'ha','wa'}, dimensions={0} | all-to-all | bytes 262144 | tf_op jit(solution)/shard_map/all_to_all | solution.py:366
  16.3 0.0 slice-done
  16.3 0.0 slice-done.1
  16.3 0.0 copy-done
  16.3 0.0 copy-done.1
  16.4 0.0 copy-done.2
  16.4 0.3 shard_map.83
  16.6 2.9 %collective-permute-start = (bf16[16,16,128]{2,1,0:T(8,128)(2,1)S(1)}, bf16[16,16,128]{2,1,0:T(8,128)(2,1)S(1)}, u32[]{:S(2)}, u32[]{:S(2)}) collective-permute-start(bf16[16,16,128]{2,1,0:T(8,128)(2,1)S(1)} %get-tuple-element.18.own_ref), channel_id=1, source_target_pairs={{0,16},{16,32},{32,48},{48,64},{64,80},{80,96},{96,112},{112,128},... | collective-permute-start | bytes 196616 | tf_op jit(solution)/shard_map/ppermute | solution.py:379
  19.5 0.0 copy-start.3
  19.5 3.4 %shard_map.84 = (bf16[2,9,384,256]{3,2,1,0:T(8,128)(2,1)S(1)}, f32[7,128,384]{2,1,0:T(8,128)S(1)}, f32[14,48,256]{2,1,0:T(8,128)S(1)}) custom-call(bf16[27,384,256]{2,1,0:T(8,128)(2,1)S(1)} %bitcast.2, bf16[27,16,384]{2,1,0:T(8,128)(2,1)S(1)} %copy-done, f32[384]{0:T(512)S(1)} %copy-done.1, ...), custom_call_target="tpu_custom_call", output_to_operand_aliasing={{0}: (6, {}), {1}: (7, {}), {2}: (8, {})} | custom-call | flops 400000000 | bytes 8000000 | tf_op jit(solution)/shard_map/pallas_call | solution.py:380
  23.0 0.5 %collective-permute-done.prev_ref = bf16[16,16,128]{2,1,0:T(8,128)(2,1)S(1)} collective-permute-done((bf16[16,16,128]{2,1,0:T(8,128)(2,1)S(1)}, bf16[16,16,128]{2,1,0:T(8,128)(2,1)S(1)}, u32[]{:S(2)}, u32[]{:S(2)}) %collective-permute-start) | collective-permute-done | bytes 65568 | tf_op jit(solution)/shard_map/ppermute | solution.py:379
  23.4 0.0 copy-done.3
  23.4 8.4 %shard_map.85 = bf16[4,12,24,256]{3,2,1,0:T(8,128)(2,1)} custom-call(bf16[16,16,128]{2,1,0:T(8,128)(2,1)S(1)} %collective-permute-done.prev_ref, bf16[16,16,128]{2,1,0:T(8,128)(2,1)S(1)} %get-tuple-element.18.own_ref, s32[24,128]{1,0:T(8,128)S(1)} %get-tuple-element.17.size_ref, bf16[27,16,384]{2,1,0:T(8,128)(2,1)S(1)} %copy-done, f32[384]{0:T(512)S(1)} %copy-done.1, ...), custom_call_target="tpu_custom_call" | custom-call | flops 4499999744 | bytes 8000000 | tf_op jit(solution)/shard_map/pallas_call | solution.py:390
  (1 shorter events, 0.0 us)
Async XLA Ops:
  0.0 16.3 %slice-start = ((s8[5308416]{0:T(1024)(128)(4,1)}), s8[4194304]{0:T(1024)(128)(4,1)S(1)}, s32[]{:S(2)}) async-start(s8[5308416]{0:T(1024)(128)(4,1)} %bitcast.1), calls=%async_computation.1 | async-start | bytes 8388608
  0.0 16.3 %slice-start.1 = ((s8[5308416]{0:T(1024)(128)(4,1)}), s8[1114112]{0:T(1024)(128)(4,1)S(1)}, s32[]{:S(2)}) async-start(s8[5308416]{0:T(1024)(128)(4,1)} %bitcast.1), calls=%async_computation.2 | async-start | bytes 2228224
  0.0 16.3 %copy-start = (bf16[27,16,384]{2,1,0:T(8,128)(2,1)S(1)}, bf16[27,16,384]{2,1,0:T(8,128)(2,1)}, u32[]{:S(2)}) copy-start(bf16[27,16,384]{2,1,0:T(8,128)(2,1)} %wi_ref.5) | copy-start | bytes 995332
  0.0 16.3 %copy-start.1 = (f32[384]{0:T(512)S(1)}, f32[384]{0:T(512)}, u32[]{:S(2)}) copy-start(f32[384]{0:T(512)} %bi_ref.5) | copy-start | bytes 4612
  0.0 16.3 %copy-start.2 = (f32[384]{0:T(512)S(1)}, f32[384]{0:T(512)}, u32[]{:S(2)}) copy-start(f32[384]{0:T(512)} %gain_ref.5) | copy-start | bytes 4612
  16.6 6.8 %collective-permute-start = (bf16[16,16,128]{2,1,0:T(8,128)(2,1)S(1)}, bf16[16,16,128]{2,1,0:T(8,128)(2,1)S(1)}, u32[]{:S(2)}, u32[]{:S(2)}) collective-permute-start(bf16[16,16,128]{2,1,0:T(8,128)(2,1)S(1)} %get-tuple-element.18.own_ref), channel_id=1, source_target_pairs={{0,16},{16,32},{32,48},{48,64},{64,80},{80,96},{96,112},{112,128},... | collective-permute-start | bytes 196616 | tf_op jit(solution)/shard_map/ppermute | solution.py:379
  19.5 3.9 %copy-start.3 = (f32[256]{0:T(256)S(1)}, f32[256]{0:T(256)}, u32[]{:S(2)}) copy-start(f32[256]{0:T(256)} %bm_ref.1) | copy-start | bytes 3076
